TPU v7x, 32 devices: a whole 2x2x4 slice. The times are simulated.
32 devices in a mesh: dp: 8 (over z, y), tensor: 4 (over x, core).
Axes of the slice: x: 2, y: 2, z: 4, core: 2. Of those that a mesh axis runs over, the one named last changes fastest.
Arguments:
- tokens: bfloat16 [8192, 768], P(('dp', 'tensor')), may hold values from -6 to 6
- out_grad: bfloat16 [8192, 768], P(('dp', 'tensor')), may hold values from -6 to 6
- segments: int32 [8, 1024], P('dp'), may hold values from 0 to 8, as said below
- neighbours: bfloat16 [128, 256, 768], P('dp'), may hold values from -6 to 6
- norm_gains: bfloat16 [3, 768], replicated, may hold values from 0.5 to 1.5
- norm_biases: bfloat16 [3, 768], replicated, may hold values from -1.25 to 1.25
- self_qkv: bfloat16 [3, 768, 768], P(None, None, 'tensor'), may hold values from -0.21875 to 0.21875
- self_out: bfloat16 [768, 768], P('tensor'), may hold values from -1.75 to 1.75
- cross_q: bfloat16 [768, 768], P(None, 'tensor'), may hold values from -0.21875 to 0.21875
- cross_kv: bfloat16 [2, 768, 768], P(None, None, 'tensor'), may hold values from -0.21875 to 0.21875
- cross_out: bfloat16 [768, 768], P('tensor'), may hold values from -1.75 to 1.75
- mlp_in: bfloat16 [768, 3072], P(None, 'tensor'), may hold values from -0.21875 to 0.21875
- mlp_in_bias: bfloat16 [3072], P('tensor'), may hold values from -1.75 to 1.75
- mlp_out: bfloat16 [3072, 768], P('tensor'), may hold values from -0.109375 to 0.109375
- mlp_out_bias: bfloat16 [768], replicated, may hold values from -1.75 to 1.75
Outputs:
- output: bfloat16 [8192, 768], P(('dp', 'tensor'))
- tokens_grad: bfloat16 [8192, 768], P(('dp', 'tensor'))
- neighbours_grad: bfloat16 [128, 256, 768], P(('dp', 'tensor'))
- norm_gains_grad: float32 [3, 768], replicated
- norm_biases_grad: float32 [3, 768], replicated
- self_qkv_grad: float32 [3, 768, 768], P(None, None, 'tensor')
- self_out_grad: float32 [768, 768], P('tensor')
- cross_q_grad: float32 [768, 768], P(None, 'tensor')
- cross_kv_grad: float32 [2, 768, 768], P(None, None, 'tensor')
- cross_out_grad: float32 [768, 768], P('tensor')
- mlp_in_grad: float32 [768, 3072], P(None, 'tensor')
- mlp_in_bias_grad: float32 [3072], P('tensor')
- mlp_out_grad: float32 [3072, 768], P('tensor')
- mlp_out_bias_grad: float32 [768], replicated
Inputs may be any that keep to these rules, and one draw needn't show every extreme that they name: `segments`: ids never fall along a sequence; every sequence has one document that starts before token 128 and ends after token 896; the last token's id is 8.
All inputs are finite; a program needn't handle non-finite values.
Results may differ from a plain program's by a relative error of at most 0.03.
Values may be sent and summed in bfloat16 or wider, within the bound.
No kernel may reach another device: no remote copies, remote signals or barrier semaphores. Data moves between devices by JAX's collectives and lax.ppermute only.
A program may use at most 128 MiB of HBM per device.

v0:
```python
import jax
import jax.numpy as jnp
from jax import lax
from jax.sharding import PartitionSpec as P

HEAD_DIM = 64
SPAN = 64


norm_epsilon = 1e-05
masked_fill = -1e30


def norm_rows(values):
    center = values - jnp.mean(values, -1, keepdims=True)
    inverse = lax.rsqrt(jnp.mean(center * center, -1, keepdims=True) + norm_epsilon)
    return (center * inverse, inverse)


def norm_back(upstream, normed, inverse, gain):
    scaled = upstream * gain
    return inverse * (
        scaled
        - jnp.mean(scaled, -1, keepdims=True)
        - normed * jnp.mean(scaled * normed, -1, keepdims=True)
    )


def rope_tables(length, dim_size):
    half_size = dim_size // 2
    places = jnp.arange(length).astype(jnp.float32)
    frequency = 10000.0 ** (-(jnp.arange(half_size).astype(jnp.float32) * 2.0 / dim_size))
    angles = places[:, None] * frequency[None, :]
    return (jnp.cos(angles)[:, None, :], jnp.sin(angles)[:, None, :])


def rotate(values, cosine, sine_part):
    half_size = values.shape[-1] // 2
    first_half = values[..., :half_size]
    second_half = values[..., half_size:]
    return jnp.concatenate(
        [
            first_half * cosine - second_half * sine_part,
            second_half * cosine + first_half * sine_part,
        ],
        -1,
    )


def unrotate(grads, cosine, sine_part):
    half_size = grads.shape[-1] // 2
    first_half = grads[..., :half_size]
    second_half = grads[..., half_size:]
    return jnp.concatenate(
        [
            first_half * cosine + second_half * sine_part,
            second_half * cosine - first_half * sine_part,
        ],
        -1,
    )


def gelu_tanh(values):
    return jax.nn.gelu(values, approximate=True)


def softmax_stats(scores):
    row_max = jnp.max(scores, -1, keepdims=True)
    expo = jnp.exp(scores - row_max)
    row_sum = jnp.sum(expo, -1, keepdims=True)
    return (expo / row_sum, (row_max + jnp.log(row_sum))[..., 0])


def local(
    tokens,
    out_grad,
    segments,
    neighbours,
    norm_gains,
    norm_biases,
    self_qkv,
    self_out,
    cross_q,
    cross_kv,
    cross_out,
    mlp_in,
    mlp_in_bias,
    mlp_out,
    mlp_out_bias,
):
    low_type = jnp.bfloat16
    wide_type = jnp.float32
    whole_tokens, whole_grads = (
        lax.all_gather(tokens, "tensor", axis=0, tiled=True),
        lax.all_gather(out_grad, "tensor", axis=0, tiled=True),
    )
    seq_len = whole_tokens.shape[0]
    row_count = tokens.shape[0]
    local_width = self_out.shape[0]
    head_count = local_width // HEAD_DIM
    own_start = lax.axis_index("tensor") * row_count
    segment = segments[0]
    gains = norm_gains.astype(wide_type)
    biases = norm_biases.astype(wide_type)
    normed_one, inverse_one = norm_rows(whole_tokens.astype(wide_type))
    input_one = (normed_one * gains[0] + biases[0]).astype(low_type)
    projected = jnp.einsum("sd,kde->kse", input_one, self_qkv, preferred_element_type=wide_type)
    cosine, sine_part = rope_tables(seq_len, HEAD_DIM)
    queries = rotate(projected[0].reshape(seq_len, head_count, HEAD_DIM), cosine, sine_part).astype(
        low_type
    )
    keys_rot = rotate(
        projected[1].reshape(seq_len, head_count, HEAD_DIM), cosine, sine_part
    ).astype(low_type)
    values = projected[2].reshape(seq_len, head_count, HEAD_DIM).astype(low_type)
    block_rows = min(512, seq_len)
    block_count = seq_len // block_rows
    key_places = jnp.arange(seq_len)

    def block_scores(first_row):
        query_block = lax.dynamic_slice_in_dim(queries, first_row, block_rows, 0)
        segment_block = lax.dynamic_slice_in_dim(segment, first_row, block_rows, 0)
        row_places = first_row + jnp.arange(block_rows)
        allowed = (row_places[:, None] >= key_places[None, :]) & (
            segment_block[:, None] == segment[None, :]
        )
        scores = (
            jnp.einsum("qhe,khe->hqk", query_block, keys_rot, preferred_element_type=wide_type)
            * 0.125
        )
        return (jnp.where(allowed[None], scores, masked_fill), allowed, query_block)

    def self_forward(block_index):
        scores, allowed, query_block = block_scores(block_index * block_rows)
        probs, log_sums = softmax_stats(scores)
        mixed = jnp.einsum(
            "hqk,khe->qhe", probs.astype(low_type), values, preferred_element_type=wide_type
        )
        return (mixed.astype(low_type), log_sums)

    attended, self_lse = lax.map(self_forward, jnp.arange(block_count))
    attended = attended.reshape(seq_len, local_width)
    branch_one = lax.psum_scatter(
        jnp.dot(attended, self_out, preferred_element_type=wide_type).astype(jnp.bfloat16),
        "tensor",
        scatter_dimension=0,
        tiled=True,
    ).astype(jnp.float32)
    resid_one = tokens.astype(wide_type) + branch_one
    normed_two, inverse_two = norm_rows(resid_one)
    input_two = lax.all_gather(
        (normed_two * gains[1] + biases[1]).astype(low_type), "tensor", axis=0, tiled=True
    )
    cross_queries = jnp.dot(input_two, cross_q, preferred_element_type=wide_type).astype(low_type)
    shift_rows = SPAN - 1
    span_count = seq_len // SPAN
    shifted = jnp.concatenate(
        [cross_queries[shift_rows:], jnp.zeros((shift_rows, local_width), low_type)], 0
    )
    shifted = shifted.reshape(span_count, SPAN, head_count, HEAD_DIM)
    nb_tokens = neighbours.shape[1]
    pool_kv = jnp.einsum(
        "pnd,kde->kpne", neighbours, cross_kv, preferred_element_type=wide_type
    ).astype(low_type)
    span_keys = pool_kv[0].reshape(span_count, nb_tokens, head_count, HEAD_DIM)
    span_values = pool_kv[1].reshape(span_count, nb_tokens, head_count, HEAD_DIM)
    cross_scores = (
        jnp.einsum("cqhe,cnhe->chqn", shifted, span_keys, preferred_element_type=wide_type) * 0.125
    )
    cross_probs, cross_lse = softmax_stats(cross_scores)
    cross_mixed = jnp.einsum(
        "chqn,cnhe->cqhe",
        cross_probs.astype(low_type),
        span_values,
        preferred_element_type=wide_type,
    )
    cross_mixed = cross_mixed.astype(low_type).reshape(seq_len, local_width)
    cross_full = jnp.concatenate(
        [jnp.zeros((shift_rows, local_width), low_type), cross_mixed[: seq_len - shift_rows]], 0
    )
    branch_two = lax.psum_scatter(
        jnp.dot(cross_full, cross_out, preferred_element_type=wide_type).astype(jnp.bfloat16),
        "tensor",
        scatter_dimension=0,
        tiled=True,
    ).astype(jnp.float32)
    resid_two = resid_one + branch_two
    normed_three, inverse_three = norm_rows(resid_two)
    input_three = lax.all_gather(
        (normed_three * gains[2] + biases[2]).astype(low_type), "tensor", axis=0, tiled=True
    )
    pre_act = jnp.dot(input_three, mlp_in, preferred_element_type=wide_type) + mlp_in_bias.astype(
        wide_type
    )
    hidden = gelu_tanh(pre_act).astype(low_type)
    branch_three = lax.psum_scatter(
        jnp.dot(hidden, mlp_out, preferred_element_type=wide_type).astype(jnp.bfloat16),
        "tensor",
        scatter_dimension=0,
        tiled=True,
    ).astype(jnp.float32)
    output = (resid_two + branch_three + mlp_out_bias.astype(wide_type)).astype(low_type)
    grad_mlp_out = jnp.einsum("sf,sd->fd", hidden, whole_grads, preferred_element_type=wide_type)
    grad_mlp_out_bias = jnp.sum(whole_grads, 0, dtype=wide_type)
    grad_hidden = jnp.einsum("sd,fd->sf", whole_grads, mlp_out, preferred_element_type=wide_type)
    gelu_pull = jax.vjp(gelu_tanh, pre_act)[1]
    grad_pre = gelu_pull(grad_hidden)[0].astype(low_type)
    grad_mlp_in = jnp.einsum("sd,sf->df", input_three, grad_pre, preferred_element_type=wide_type)
    grad_mlp_in_bias = jnp.sum(grad_pre, 0, dtype=wide_type)
    grad_norm_three = lax.psum_scatter(
        jnp.einsum("sf,df->sd", grad_pre, mlp_in, preferred_element_type=wide_type).astype(
            jnp.bfloat16
        ),
        "tensor",
        scatter_dimension=0,
        tiled=True,
    ).astype(jnp.float32)
    grads_two = out_grad.astype(wide_type) + norm_back(
        grad_norm_three, normed_three, inverse_three, gains[2]
    )
    gain_three = jnp.sum(grad_norm_three * normed_three, 0)
    bias_three = jnp.sum(grad_norm_three, 0)
    grads_two_whole = lax.all_gather(grads_two.astype(low_type), "tensor", axis=0, tiled=True)
    grad_cross_out = jnp.einsum(
        "se,sd->ed", cross_full, grads_two_whole, preferred_element_type=wide_type
    )
    grad_cross_full = jnp.einsum(
        "sd,ed->se", grads_two_whole, cross_out, preferred_element_type=wide_type
    ).astype(low_type)
    grad_cross_mixed = jnp.concatenate(
        [grad_cross_full[shift_rows:], jnp.zeros((shift_rows, local_width), low_type)], 0
    )
    grad_cross_mixed = grad_cross_mixed.reshape(span_count, SPAN, head_count, HEAD_DIM)
    cross_again = (
        jnp.einsum("cqhe,cnhe->chqn", shifted, span_keys, preferred_element_type=wide_type) * 0.125
    )
    cross_back = jnp.exp(cross_again - cross_lse[..., None])
    grad_cross_probs = jnp.einsum(
        "cqhe,cnhe->chqn", grad_cross_mixed, span_values, preferred_element_type=wide_type
    )
    cross_inner = jnp.sum(cross_back * grad_cross_probs, -1, keepdims=True)
    grad_cross_scores = (cross_back * (grad_cross_probs - cross_inner)).astype(low_type)
    grad_shifted = (
        jnp.einsum(
            "chqn,cnhe->cqhe", grad_cross_scores, span_keys, preferred_element_type=wide_type
        )
        * 0.125
    )
    grad_span_keys = (
        jnp.einsum("chqn,cqhe->cnhe", grad_cross_scores, shifted, preferred_element_type=wide_type)
        * 0.125
    )
    grad_span_values = jnp.einsum(
        "chqn,cqhe->cnhe",
        cross_back.astype(low_type),
        grad_cross_mixed,
        preferred_element_type=wide_type,
    )
    grad_pool = (
        jnp.stack([grad_span_keys, grad_span_values])
        .reshape(2, span_count, nb_tokens, local_width)
        .astype(low_type)
    )
    grad_cross_kv = jnp.einsum(
        "pnd,kpne->kde", neighbours, grad_pool, preferred_element_type=wide_type
    )
    grad_cross_queries = jnp.concatenate(
        [
            jnp.zeros((shift_rows, local_width), wide_type),
            grad_shifted.reshape(seq_len, local_width)[: seq_len - shift_rows],
        ],
        0,
    )
    grad_cross_queries = grad_cross_queries.astype(low_type)
    grad_cross_q = jnp.einsum(
        "sd,se->de", input_two, grad_cross_queries, preferred_element_type=wide_type
    )
    grad_two_part = jnp.einsum(
        "se,de->sd", grad_cross_queries, cross_q, preferred_element_type=wide_type
    )
    grad_nb_part = jnp.einsum(
        "kpne,kde->pnd", grad_pool, cross_kv, preferred_element_type=wide_type
    )
    grad_norm_two, grad_nb = (
        lax.psum_scatter(
            grad_two_part.astype(jnp.bfloat16), "tensor", scatter_dimension=0, tiled=True
        ).astype(jnp.float32),
        lax.psum_scatter(
            grad_nb_part.astype(jnp.bfloat16), "tensor", scatter_dimension=0, tiled=True
        ).astype(jnp.float32),
    )
    neighbours_grad = grad_nb.astype(low_type)
    grads_one = grads_two + norm_back(grad_norm_two, normed_two, inverse_two, gains[1])
    gain_two = jnp.sum(grad_norm_two * normed_two, 0)
    bias_two = jnp.sum(grad_norm_two, 0)
    grads_one_whole = lax.all_gather(grads_one.astype(low_type), "tensor", axis=0, tiled=True)
    grad_self_out = jnp.einsum(
        "se,sd->ed", attended, grads_one_whole, preferred_element_type=wide_type
    )
    grad_attended = jnp.einsum(
        "sd,ed->se", grads_one_whole, self_out, preferred_element_type=wide_type
    ).astype(low_type)
    grad_attended = grad_attended.reshape(seq_len, head_count, HEAD_DIM)

    def self_backward(carry, block_index):
        key_total, value_total = carry
        first_row = block_index * block_rows
        scores, allowed, query_block = block_scores(first_row)
        probs = jnp.where(allowed[None], jnp.exp(scores - self_lse[block_index][:, :, None]), 0.0)
        upstream = lax.dynamic_slice_in_dim(grad_attended, first_row, block_rows, 0)
        grad_probs = jnp.einsum("qhe,khe->hqk", upstream, values, preferred_element_type=wide_type)
        inner_sum = jnp.sum(probs * grad_probs, -1, keepdims=True)
        grad_scores = (probs * (grad_probs - inner_sum)).astype(low_type)
        grad_query = (
            jnp.einsum("hqk,khe->qhe", grad_scores, keys_rot, preferred_element_type=wide_type)
            * 0.125
        )
        key_total = (
            key_total
            + jnp.einsum("hqk,qhe->khe", grad_scores, query_block, preferred_element_type=wide_type)
            * 0.125
        )
        value_total = value_total + jnp.einsum(
            "hqk,qhe->khe", probs.astype(low_type), upstream, preferred_element_type=wide_type
        )
        return ((key_total, value_total), grad_query)

    zero_grads = jnp.zeros((seq_len, head_count, HEAD_DIM), wide_type)
    (key_grads, value_grads), query_grads = lax.scan(
        self_backward, (zero_grads, zero_grads), jnp.arange(block_count)
    )
    query_grads = query_grads.reshape(seq_len, head_count, HEAD_DIM)
    grad_projected = jnp.stack(
        [
            unrotate(query_grads, cosine, sine_part).astype(low_type),
            unrotate(key_grads, cosine, sine_part).astype(low_type),
            value_grads.astype(low_type),
        ]
    )
    grad_projected = grad_projected.reshape(3, seq_len, local_width)
    grad_self_qkv = jnp.einsum(
        "sd,kse->kde", input_one, grad_projected, preferred_element_type=wide_type
    )
    own_grad = lax.psum_scatter(
        jnp.einsum(
            "kse,kde->sd", grad_projected, self_qkv, preferred_element_type=wide_type
        ).astype(jnp.bfloat16),
        "tensor",
        scatter_dimension=0,
        tiled=True,
    ).astype(jnp.float32)
    own_normed = lax.dynamic_slice_in_dim(normed_one, own_start, row_count, 0)
    own_inverse = lax.dynamic_slice_in_dim(inverse_one, own_start, row_count, 0)
    tokens_grad = (grads_one + norm_back(own_grad, own_normed, own_inverse, gains[0])).astype(
        low_type
    )
    gain_one = jnp.sum(own_grad * own_normed, 0)
    bias_one = jnp.sum(own_grad, 0)
    gain_parts = jnp.stack([gain_one, gain_two, gain_three])
    bias_parts = jnp.stack([bias_one, bias_two, bias_three])
    gain_parts, bias_parts = lax.psum((gain_parts, bias_parts), ("dp", "tensor"))
    (
        grad_self_qkv,
        grad_self_out,
        grad_mlp_in,
        grad_mlp_in_bias,
        grad_mlp_out,
        grad_mlp_out_bias,
        grad_cross_q,
        grad_cross_kv,
        grad_cross_out,
    ) = lax.psum(
        (
            grad_self_qkv,
            grad_self_out,
            grad_mlp_in,
            grad_mlp_in_bias,
            grad_mlp_out,
            grad_mlp_out_bias,
            grad_cross_q,
            grad_cross_kv,
            grad_cross_out,
        ),
        "dp",
    )
    return (
        output,
        tokens_grad,
        neighbours_grad,
        gain_parts,
        bias_parts,
        grad_self_qkv,
        grad_self_out,
        grad_cross_q,
        grad_cross_kv,
        grad_cross_out,
        grad_mlp_in,
        grad_mlp_in_bias,
        grad_mlp_out,
        grad_mlp_out_bias,
    )


def solution(mesh):
    in_specs = (
        P(("dp", "tensor"), None),
        P(("dp", "tensor"), None),
        P("dp", None),
        P("dp", None, None),
        P(),
        P(),
        P(None, None, "tensor"),
        P("tensor", None),
        P(None, "tensor"),
        P(None, None, "tensor"),
        P("tensor", None),
        P(None, "tensor"),
        P("tensor"),
        P("tensor", None),
        P(),
    )
    out_specs = (
        P(("dp", "tensor"), None),
        P(("dp", "tensor"), None),
        P(("dp", "tensor"), None, None),
        P(),
        P(),
        P(None, None, "tensor"),
        P("tensor", None),
        P(None, "tensor"),
        P(None, None, "tensor"),
        P("tensor", None),
        P(None, "tensor"),
        P("tensor"),
        P("tensor", None),
        P(),
    )
    return jax.shard_map(local, mesh=mesh, in_specs=in_specs, out_specs=out_specs, check_vma=False)
```

profile of v0, /device:TPU:0, one launch (start us, length us, event | category | flops | bytes accessed | tf_op | source)
XLA Modules:
  0.0 826.4 jit_solution(13038336341598157848)
XLA Ops:
  10.6 21.4 %all-gather.7.cloned.1.call-done = bf16[1024,768]{1,0:T(8,128)(2,1)} async-done(((bf16[256,768]{1,0:T(8,128)(2,1)}), bf16[1024,768]{1,0:T(8,128)(2,1)}) %all-gather.7.cloned.1.call-update) | async-done | bytes 1572880 | tf_op jit(solution)/shard_map/all_gather | solution.py:94
  39.3 18.4 %while.28 = (s32[]{:T(128)}, bf16[2,512,3,64]{1,3,2,0:T(8,128)(2,1)S(1)}, f32[2,3,512]{2,1,0:T(4,128)S(1)}, s32[2]{0:T(128)S(1)}, s32[1024]{0:T(1024)S(1)}, /*in...) while((s32[]{:T(128)}, ...), condition=%wide.region_5.6_spmd.clone, body=%wide.region_2.5_spmd.clone.sunk | while | flops 423197696 | bytes 22225108 | solution.py:141
  41.1 2.3 fusion.203
  45.2 3.2 fusion.205
  50.3 2.3 fusion.203
  54.4 3.2 fusion.205
  60.0 28.3 %reduce-scatter.8.cloned.1.call-done = bf16[256,768]{1,0:T(8,128)(2,1)} async-done(((bf16[1024,768]{1,0:T(8,128)(2,1)}), bf16[256,768]{1,0:T(8,128)(2,1)}) %reduce-scatter.8.cloned.1.call-update) | async-done | bytes 393232 | tf_op jit(solution)/shard_map/reduce_scatter | solution.py:143
  93.3 7.2 convert_bitcast_fusion
  102.5 10.1 %all-gather.9.cloned.1.call-done = bf16[1024,768]{1,0:T(8,128)(2,1)} async-done(((bf16[256,768]{1,0:T(8,128)(2,1)}), bf16[1024,768]{1,0:T(8,128)(2,1)}) %all-gather.9.cloned.1.call-update) | async-done | bytes 1572880 | tf_op jit(solution)/shard_map/all_gather | solution.py:151
  115.4 2.5 multiply_reduce_fusion.2
  122.5 3.1 convolution_convert_fusion.4
  125.6 28.3 %reduce-scatter.10.cloned.1.call-done = bf16[256,768]{1,0:T(8,128)(2,1)} async-done(((bf16[1024,768]{1,0:T(8,128)(2,1)}), bf16[256,768]{1,0:T(8,128)(2,1)}) %reduce-scatter.10.cloned.1.call-update) | async-done | bytes 393232 | tf_op jit(solution)/shard_map/reduce_scatter | solution.py:181
  158.3 18.5 %all-gather.11.cloned.1.call-done = bf16[1024,768]{1,0:T(8,128)(2,1)} async-done(((bf16[256,768]{1,0:T(8,128)(2,1)}), bf16[1024,768]{1,0:T(8,128)(2,1)}) %all-gather.11.cloned.1.call-update) | async-done | bytes 1572880 | tf_op jit(solution)/shard_map/all_gather | solution.py:189
  176.8 4.9 fusion.137
  181.7 16.3 %all-gather.13.cloned.1.call-done = bf16[1024,768]{1,0:T(8,128)(2,1)} async-done(((bf16[256,768]{1,0:T(8,128)(2,1)}), bf16[1024,768]{1,0:T(8,128)(2,1)}) %all-gather.13.cloned.1.call-update) | async-done | bytes 1572880 | tf_op jit(solution)/shard_map/all_gather | solution.py:95
  198.0 6.3 convert_reduce_fusion.2
  205.3 2.6 convolution_convert_fusion.2
  208.2 5.1 convolution_convert_fusion.3
  213.4 22.8 %reduce-scatter.14.cloned.1.call-done = bf16[256,768]{1,0:T(8,128)(2,1)} async-done(((bf16[1024,768]{1,0:T(8,128)(2,1)}), bf16[256,768]{1,0:T(8,128)(2,1)}) %reduce-scatter.14.cloned.1.call-update) | async-done | bytes 393232 | tf_op jit(solution)/shard_map/reduce_scatter | solution.py:210
  238.3 29.5 %reduce-scatter.12.cloned.1.call-done = bf16[256,768]{1,0:T(8,128)(2,1)} async-done(((bf16[1024,768]{1,0:T(8,128)(2,1)}), bf16[256,768]{1,0:T(8,128)(2,1)}) %reduce-scatter.12.cloned.1.call-update) | async-done | bytes 393232 | tf_op jit(solution)/shard_map/reduce_scatter | solution.py:196
  267.7 2.6 fusion.131
  272.0 18.2 %all-gather.15.cloned.1.call-done = bf16[1024,768]{1,0:T(8,128)(2,1)} async-done(((bf16[256,768]{1,0:T(8,128)(2,1)}), bf16[1024,768]{1,0:T(8,128)(2,1)}) %all-gather.15.cloned.1.call-update) | async-done | bytes 1572880 | tf_op jit(solution)/shard_map/all_gather | solution.py:223
  293.3 2.4 reshape.391
  295.7 3.1 multiply_reduce_fusion.1
  304.5 28.3 %reduce-scatter.16.cloned.1.call-done = bf16[256,768]{1,0:T(8,128)(2,1)} async-done(((bf16[1024,768]{1,0:T(8,128)(2,1)}), bf16[256,768]{1,0:T(8,128)(2,1)}) %reduce-scatter.16.cloned.1.call-update) | async-done | bytes 393232 | tf_op jit(solution)/shard_map/reduce_scatter | solution.py:285
  334.8 2.4 fusion.129
  337.5 19.5 %all-gather.17.cloned.1.call-done = bf16[1024,768]{1,0:T(8,128)(2,1)} async-done(((bf16[256,768]{1,0:T(8,128)(2,1)}), bf16[1024,768]{1,0:T(8,128)(2,1)}) %all-gather.17.cloned.1.call-update) | async-done | bytes 1572880 | tf_op jit(solution)/shard_map/all_gather | solution.py:296
  357.0 2.8 convolution_convert_fusion.6
  359.8 41.8 %while.29 = (s32[]{:T(128)}, f32[1024,3,64]{0,2,1:T(8,128)S(1)}, f32[1024,3,64]{0,2,1:T(8,128)}, f32[2,512,3,64]{1,0,3,2:T(2,128)}, s32[2]{0:T(128)S(1)}, /*inde...) while((s32[]{:T(128)}, f32[1024,3,64]{0,2,1:T(8,128)S(1)}, ...), condition=%wide.region_24.25_spmd.clone, body=%wide.region_22.24_spmd.clone.sunk | while | flops 1025014784 | bytes 63222140 | solution.py:329
  363.6 2.1 fusion.215
  365.7 4.1 multiply_reduce_fusion.6
  375.6 3.6 dynamic_update_slice.22
  386.0 4.1 multiply_reduce_fusion.6
  391.1 2.7 fusion.218
  397.1 3.6 dynamic_update_slice.22
  407.0 2.6 bitcast_convert_fusion.1
  409.7 2.4 multiply_convert_fusion.1
  414.7 5.4 bitcast_convert_fusion
  420.4 4.9 fusion.140
  425.3 5.6 fusion.125
  433.8 3.7 fusion.65
  438.8 2.6 fusion.61
  441.8 2.2 fusion.41
  444.0 22.2 %all-reduce.5 = (f32[768]{0:T(1024)}, f32[768]{0:T(1024)}) all-reduce(f32[768]{0:T(1024)S(1)} %copy-done.75, f32[768]{0:T(1024)S(1)} %convert_reduce_fusion.1), channel_id=1, replica_groups=mesh['dp'=8,'tensor'=4] {'dp'}, use_global_device_ids=true, to_apply=%region_44.45 | all-reduce | flops 1536 | bytes 12288 | tf_op jit(solution)/shard_map/psum | solution.py:372
  467.9 37.7 %all-reduce.4 = (f32[3,768]{1,0:T(4,128)}, f32[3,768]{1,0:T(4,128)}) all-reduce(f32[3,768]{1,0:T(4,128)S(1)} %pad_maximum_fusion.12, f32[3,768]{1,0:T(4,128)S(1)} %pad_maximum_fusion.13), channel_id=1, replica_groups=mesh['dp'=8,'tensor'=4] {'dp','tensor'}, use_global_device_ids=true, to_apply=%region_32.33 | all-reduce | flops 4608 | bytes 36864 | tf_op jit(solution)/shard_map/psum | solution.py:361
  505.6 2.2 fusion.82
  507.9 302.3 %all-reduce.9.cloned.1.call-done = (f32[3,768,192]{1,2,0:T(8,128)}, f32[192,768]{1,0:T(8,128)}, f32[768,192]{0,1:T(8,128)}, f32[2,768,192]{1,2,0:T(8,128)}, f32[...) async-done(((f32[3,768,192]{1,2,0:T(8,128)}, f32[192,768]{1,0:T(8,128)}, f32[768,192]{0,1:T(8,128)}, f32[2,768,192]{1,2,0:T(8,128)}, f32[192,768]{1,0:T(8,128)}, ...) | async-done | bytes 9437200 | tf_op jit(solution)/shard_map/psum | solution.py:372
  810.2 2.9 copy.121
  (333 shorter events, 90.5 us)
Async XLA Ops:
  7.2 190.8 %copy-start = (bf16[768,768]{1,0:T(8,128)(2,1)S(1)}, bf16[768,768]{1,0:T(8,128)(2,1)}, u32[]{:S(2)}) copy-start(bf16[768,768]{1,0:T(8,128)(2,1)} %param.32) | copy-start | bytes 3538948
  7.2 28.7 %copy-start.80 = (bf16[3,768,192]{1,2,0:T(8,128)(2,1)S(1)}, bf16[3,768,192]{1,2,0:T(8,128)(2,1)}, u32[]{:S(2)}) copy-start(bf16[3,768,192]{1,2,0:T(8,128)(2,1)} %param.25) | copy-start | bytes 2654212
  7.2 24.8 %all-gather.7.cloned.1.call-start = ((), (), s32[]{:S(2)}) async-start(), calls=%async_computation.7 | async-start | bytes 1966080 | tf_op jit(solution)/shard_map/all_gather | solution.py:94
  7.9 80.4 %reduce-scatter.8.cloned.1.call-start = ((), (), s32[]{:S(2)}) async-start(), calls=%async_computation.8 | async-start | bytes 1966080 | tf_op jit(solution)/shard_map/reduce_scatter | solution.py:143
  10.0 27.2 %copy-start.63 = (f32[768]{0:T(1024)}, f32[768]{0:T(1024)S(1)}, u32[]{:S(2)}) copy-start(f32[768]{0:T(1024)S(1)} %get-tuple-element.308) | copy-start | bytes 9220
  10.0 27.2 %copy-start.76 = (f32[768]{0:T(1024)}, f32[768]{0:T(1024)S(1)}, u32[]{:S(2)}) copy-start(f32[768]{0:T(1024)S(1)} %get-tuple-element.219) | copy-start | bytes 9220
  10.6 27.6 %copy-start.36 = (f32[1024,32]{0,1:T(8,128)}, f32[1024,32]{0,1:T(8,128)S(1)}, u32[]{:S(2)}) copy-start(f32[1024,32]{0,1:T(8,128)S(1)} %get-tuple-element.302) | copy-start | bytes 393220
  10.6 27.6 %copy-start.37 = (f32[1024,32]{0,1:T(8,128)}, f32[1024,32]{0,1:T(8,128)S(1)}, u32[]{:S(2)}) copy-start(f32[1024,32]{0,1:T(8,128)S(1)} %get-tuple-element.303) | copy-start | bytes 393220
  39.3 18.9 %copy-start.56 = (bf16[192,768]{1,0:T(8,128)(2,1)S(1)}, bf16[192,768]{1,0:T(8,128)(2,1)}, u32[]{:S(2)}) copy-start(bf16[192,768]{1,0:T(8,128)(2,1)} %param.26) | copy-start | bytes 884740
  57.7 33.1 %copy-start.59 = (f32[2,3,512]{2,1,0:T(4,128)}, f32[2,3,512]{2,1,0:T(4,128)S(1)}, u32[]{:S(2)}) copy-start(f32[2,3,512]{2,1,0:T(4,128)S(1)} %get-tuple-element.495) | copy-start | bytes 36868
  57.7 30.6 %copy-start.5 = (bf16[256,768]{1,0:T(8,128)(2,1)S(1)}, bf16[256,768]{1,0:T(8,128)(2,1)}, u32[]{:S(2)}) copy-start(bf16[256,768]{1,0:T(8,128)(2,1)} %param.19) | copy-start | bytes 1179652
  58.2 34.6 %copy-start.17 = (bf16[24,8,2,512]{3,1,2,0:T(8,128)(2,1)}, bf16[24,8,2,512]{3,1,2,0:T(8,128)(2,1)S(1)}, u32[]{:S(2)}) copy-start(bf16[24,8,2,512]{3,1,2,0:T(8,128)(2,1)S(1)} %copy.75) | copy-start | bytes 1179652
  60.0 33.3 %copy-start.82 = (bf16[2,768,192]{1,2,0:T(8,128)(2,1)S(1)}, bf16[2,768,192]{1,2,0:T(8,128)(2,1)}, u32[]{:S(2)}) copy-start(bf16[2,768,192]{1,2,0:T(8,128)(2,1)} %param.28) | copy-start | bytes 1769476
  60.0 52.6 %all-gather.9.cloned.1.call-start = ((), (), s32[]{:S(2)}) async-start(), calls=%async_computation.9 | async-start | bytes 1966080 | tf_op jit(solution)/shard_map/all_gather | solution.py:151
  90.8 9.7 %copy-start.67 = (f32[256]{0:T(256)}, f32[256]{0:T(256)S(1)}, u32[]{:S(2)}) copy-start(f32[256]{0:T(256)S(1)} %add_rsqrt_fusion.2) | copy-start | bytes 3076
  92.8 61.1 %reduce-scatter.10.cloned.1.call-start = ((), (), s32[]{:S(2)}) async-start(), calls=%async_computation.10 | async-start | bytes 1966080 | tf_op jit(solution)/shard_map/reduce_scatter | solution.py:181
  100.5 12.1 %copy-start.54 = (bf16[768,192]{0,1:T(8,128)(2,1)S(1)}, bf16[768,192]{0,1:T(8,128)(2,1)}, u32[]{:S(2)}) copy-start(bf16[768,192]{0,1:T(8,128)(2,1)} %param.27) | copy-start | bytes 884740
  121.4 32.5 %copy-start.9 = (bf16[256,768]{1,0:T(8,128)(2,1)S(1)}, bf16[256,768]{1,0:T(8,128)(2,1)}, u32[]{:S(2)}) copy-start(bf16[256,768]{1,0:T(8,128)(2,1)} %reduce-scatter.8.cloned.1.call-done) | copy-start | bytes 1179652
  122.5 32.9 %copy-start.19 = (bf16[1024,192]{0,1:T(8,128)(2,1)}, bf16[1024,192]{0,1:T(8,128)(2,1)S(1)}, u32[]{:S(2)}) copy-start(bf16[1024,192]{0,1:T(8,128)(2,1)S(1)} %reshape.390) | copy-start | bytes 1179652
  125.6 51.3 %all-gather.11.cloned.1.call-start = ((), (), s32[]{:S(2)}) async-start(), calls=%async_computation.11 | async-start | bytes 1966080 | tf_op jit(solution)/shard_map/all_gather | solution.py:189
  157.0 40.9 %all-gather.13.cloned.1.call-start = ((), (), s32[]{:S(2)}) async-start(), calls=%async_computation.13 | async-start | bytes 1966080 | tf_op jit(solution)/shard_map/all_gather | solution.py:95
  157.6 78.6 %reduce-scatter.14.cloned.1.call-start = ((), (), s32[]{:S(2)}) async-start(), calls=%async_computation.14 | async-start | bytes 1966080 | tf_op jit(solution)/shard_map/reduce_scatter | solution.py:210
  158.3 49.9 %copy-start.73 = (f32[768]{0:T(1024)}, f32[768]{0:T(1024)S(1)}, u32[]{:S(2)}) copy-start(f32[768]{0:T(1024)S(1)} %convert_element_type.269) | copy-start | bytes 9220
  197.9 7.4 copy-start.79
  208.0 59.8 %copy-start.35 = (bf16[256,768]{1,0:T(8,128)(2,1)S(1)}, bf16[256,768]{1,0:T(8,128)(2,1)}, u32[]{:S(2)}) copy-start(bf16[256,768]{1,0:T(8,128)(2,1)} %param.20) | copy-start | bytes 1179652
  208.0 59.8 %reduce-scatter.12.cloned.1.call-start = ((), (), s32[]{:S(2)}) async-start(), calls=%async_computation.12 | async-start | bytes 1966080 | tf_op jit(solution)/shard_map/reduce_scatter | solution.py:196
  213.4 76.9 %all-gather.15.cloned.1.call-start = ((), (), s32[]{:S(2)}) async-start(), calls=%async_computation.15 | async-start | bytes 1966080 | tf_op jit(solution)/shard_map/all_gather | solution.py:223
  270.4 25.3 %copy-start.3 = (f32[16,3,64,256]{3,2,1,0:T(8,128)S(1)}, f32[16,3,64,256]{3,2,1,0:T(8,128)}, u32[]{:S(2)}) copy-start(f32[16,3,64,256]{3,2,1,0:T(8,128)} %copy-done.2) | copy-start | bytes 9437188
  270.4 62.3 %reduce-scatter.16.cloned.1.call-start = ((), (), s32[]{:S(2)}) async-start(), calls=%async_computation.16 | async-start | bytes 1966080 | tf_op jit(solution)/shard_map/reduce_scatter | solution.py:285
  301.3 31.4 %copy-start.6 = (bf16[256,768]{1,0:T(8,128)(2,1)S(1)}, bf16[256,768]{1,0:T(8,128)(2,1)}, u32[]{:S(2)}) copy-start(bf16[256,768]{1,0:T(8,128)(2,1)} %param.19) | copy-start | bytes 1179652
  301.3 31.4 %copy-start.10 = (bf16[256,768]{1,0:T(8,128)(2,1)S(1)}, bf16[256,768]{1,0:T(8,128)(2,1)}, u32[]{:S(2)}) copy-start(bf16[256,768]{1,0:T(8,128)(2,1)} %reduce-scatter.8.cloned.1.call-done) | copy-start | bytes 1179652
  301.3 31.4 %copy-start.68 = (f32[256]{0:T(256)S(1)}, f32[256]{0:T(256)}, u32[]{:S(2)}) copy-start(f32[256]{0:T(256)} %copy-done.67) | copy-start | bytes 3076
  301.9 32.9 %copy-start.24 = (f32[256,768]{1,0:T(8,128)S(1)}, f32[256,768]{1,0:T(8,128)}, u32[]{:S(2)}) copy-start(f32[256,768]{1,0:T(8,128)} %get-tuple-element.278) | copy-start | bytes 2359300
  302.4 34.7 %copy-start.21 = (bf16[1024,192]{0,1:T(8,128)(2,1)}, bf16[1024,192]{0,1:T(8,128)(2,1)S(1)}, u32[]{:S(2)}) copy-start(bf16[1024,192]{0,1:T(8,128)(2,1)S(1)} %reshape.392) | copy-start | bytes 1179652
  304.4 52.6 %copy-start.57 = (bf16[192,768]{1,0:T(8,128)(2,1)S(1)}, bf16[192,768]{1,0:T(8,128)(2,1)}, u32[]{:S(2)}) copy-start(bf16[192,768]{1,0:T(8,128)(2,1)} %param.26) | copy-start | bytes 884740
  304.4 52.6 %all-gather.17.cloned.1.call-start = ((), (), s32[]{:S(2)}) async-start(), calls=%async_computation.17 | async-start | bytes 1966080 | tf_op jit(solution)/shard_map/all_gather | solution.py:296
  334.8 25.0 %copy-start.60 = (f32[2,3,512]{2,1,0:T(4,128)S(1)}, f32[2,3,512]{2,1,0:T(4,128)}, u32[]{:S(2)}) copy-start(f32[2,3,512]{2,1,0:T(4,128)} %copy-done.59) | copy-start | bytes 36868
  337.2 129.1 %reduce-scatter.18.cloned.1.call-start = ((), (), s32[]{:S(2)}) async-start(), calls=%async_computation.18 | async-start | bytes 1966080 | tf_op jit(solution)/shard_map/reduce_scatter | solution.py:344
  409.6 98.2 %reduce-scatter.20.cloned.1.call-start = ((), (), s32[]{:S(2)}) async-start(), calls=%async_computation.19 | async-start | bytes 7864320 | tf_op jit(solution)/shard_map/reduce_scatter | solution.py:288
  420.1 390.1 %all-reduce.9.cloned.1.call-start = ((), (), s32[]{:S(2)}) async-start(), calls=%async_computation.20 | async-start | bytes 18874368 | tf_op jit(solution)/shard_map/psum | solution.py:372
  420.4 13.3 %slice-start = ((s8[6291456]{0:T(1024)(128)(4,1)}), s8[4194304]{0:T(1024)(128)(4,1)S(1)}, s32[]{:S(2)}) async-start(s8[6291456]{0:T(1024)(128)(4,1)} %bitcast.228), calls=%async_computation.21 | async-start | bytes 8388608
  425.3 7.0 copy-start.22
  425.3 8.3 %slice-start.1 = ((s8[6291456]{0:T(1024)(128)(4,1)}), s8[2097152]{0:T(1024)(128)(4,1)S(1)}, s32[]{:S(2)}) async-start(s8[6291456]{0:T(1024)(128)(4,1)} %bitcast.228), calls=%async_computation.22 | async-start | bytes 4194304
  441.5 24.7 %copy-start.70 = (f32[768]{0:T(1024)S(1)}, f32[768]{0:T(1024)}, u32[]{:S(2)}) copy-start(f32[768]{0:T(1024)} %get-tuple-element.206) | copy-start | bytes 9220
  441.5 24.7 %copy-start.69 = (f32[768]{0:T(1024)S(1)}, f32[768]{0:T(1024)}, u32[]{:S(2)}) copy-start(f32[768]{0:T(1024)} %get-tuple-element.213) | copy-start | bytes 9220
  441.5 24.7 %copy-start.72 = (f32[768]{0:T(1024)S(1)}, f32[768]{0:T(1024)}, u32[]{:S(2)}) copy-start(f32[768]{0:T(1024)} %get-tuple-element.204) | copy-start | bytes 9220
  441.5 24.7 %copy-start.71 = (f32[768]{0:T(1024)S(1)}, f32[768]{0:T(1024)}, u32[]{:S(2)}) copy-start(f32[768]{0:T(1024)} %get-tuple-element.212) | copy-start | bytes 9220
  441.8 63.8 %copy-start.23 = (f32[256,768]{1,0:T(8,128)S(1)}, f32[256,768]{1,0:T(8,128)}, u32[]{:S(2)}) copy-start(f32[256,768]{1,0:T(8,128)} %get-tuple-element.276) | copy-start | bytes 2359300
  (56 other events, 173.6 us)
Sparse Core Ops, SparseCore 0:
  9.6 22.3 all-gather.6
  60.1 28.1 reduce-scatter.7
  92.9 19.6 all-gather.8
  125.7 28.1 reduce-scatter.9
  157.1 19.6 all-gather.10
  178.2 19.6 all-gather.12
  208.1 28.1 reduce-scatter.13
  239.5 28.1 reduce-scatter.11
  270.5 19.6 all-gather.14
  304.5 28.1 reduce-scatter.15
  337.3 19.6 all-gather.16
  409.8 28.1 reduce-scatter.17
  441.1 59.1 reduce-scatter.19
  507.6 302.5 all-reduce.8
where the time goes:
time: 834 us; the launch traced here: 826 us
  waiting for transfers between devices  545 us (65%)
  matrix products  114 us (14%)
  blocking collectives  59.9 us (7%)
  other arithmetic  43.6 us (5%)
  local copies, waits for them, and re-layouts  40 us (5%)
  between operations  15.4 us (2%)
    psum x1, waiting for transfers between devices, local(): lax.psum((grad_self_qkv, grad_self_out, grad_mlp_in, grad_mlp_in_bias, gr...  302 us
    psum x1, blocking collectives, local(): lax.psum((gain_parts, bias_parts), ('dp', 'tensor'))  37.7 us
    reduce_scatter x1, waiting for transfers between devices, local(): lax.psum_scatter(jnp.dot(hidden, mlp_out, preferred_element_type=wide_typ...  29.5 us
    reduce_scatter x1, waiting for transfers between devices, local(): lax.psum_scatter(jnp.dot(cross_full, cross_out, preferred_element_type=wi...  28.3 us
    reduce_scatter x1, waiting for transfers between devices, local(): lax.psum_scatter(jnp.dot(attended, self_out, preferred_element_type=wide_...  28.3 us
    reduce_scatter x1, waiting for transfers between devices, local(): lax.psum_scatter(grad_two_part.astype(jnp.bfloat16), 'tensor', scatter_di...  28.3 us
    reduce_scatter x1, waiting for transfers between devices, local(): lax.psum_scatter(jnp.einsum('sf,df->sd', grad_pre, mlp_in, preferred_elem...  22.8 us
    psum x1, blocking collectives, local(): lax.psum((grad_self_qkv, grad_self_out, grad_mlp_in, grad_mlp_in_bias, gr...  22.2 us
  transfers between devices with their start and end apart: 14, of which 12 were waited for; matrix products, arithmetic and copies ran while one was open for 7% of the time, Pallas kernels for 0%

commit v1 on v0

v1 whole, which is shorter than its diff:
```python
import jax
import jax.numpy as jnp
from jax import lax
from jax.sharding import PartitionSpec as P

HEAD_DIM = 64
SPAN = 64
EPS = 1e-05
MASKED = -1e30
BF = jnp.bfloat16
F32 = jnp.float32


def norm_rows(values):
    center = values - jnp.mean(values, -1, keepdims=True)
    inverse = lax.rsqrt(jnp.mean(center * center, -1, keepdims=True) + EPS)
    return center * inverse, inverse


def norm_back(upstream, normed, inverse, gain):
    scaled = upstream * gain
    return inverse * (
        scaled
        - jnp.mean(scaled, -1, keepdims=True)
        - normed * jnp.mean(scaled * normed, -1, keepdims=True)
    )


def rope_tables(length):
    half = HEAD_DIM // 2
    places = jnp.arange(length).astype(F32)
    frequency = 10000.0 ** (-(jnp.arange(half).astype(F32) * 2.0 / HEAD_DIM))
    angles = places[:, None] * frequency[None, :]
    return jnp.cos(angles)[:, None, :], jnp.sin(angles)[:, None, :]


def rotate(values, cosine, sine):
    half = values.shape[-1] // 2
    first, second = values[..., :half], values[..., half:]
    return jnp.concatenate(
        [first * cosine - second * sine, second * cosine + first * sine], -1
    )


def gelu_tanh(values):
    return jax.nn.gelu(values, approximate=True)


def nn(left, right):
    return jnp.dot(left, right, preferred_element_type=F32)


def nt(left, right):
    return lax.dot_general(left, right, (((1,), (1,)), ((), ())), preferred_element_type=F32)


def tn(left, right):
    return lax.dot_general(left, right, (((0,), (0,)), ((), ())), preferred_element_type=F32)


def swap(value, axis, bit, size):
    return lax.ppermute(value, axis, [(i, i ^ bit) for i in range(size)])


def core_swap(value):
    return swap(value, "tensor", 1, 4)


def x_swap(value):
    return swap(value, "tensor", 2, 4)


def gather_blocks(block):
    far = x_swap(block)
    return [block, core_swap(block), far, core_swap(far)]


def scatter_sum(blocks):
    send = jnp.concatenate([blocks[1], blocks[3]], 0)
    got = core_swap(send)
    rows = blocks[0].shape[0]
    far = (blocks[2].astype(F32) + got[rows:].astype(F32)).astype(BF)
    far = x_swap(far)
    return blocks[0].astype(F32) + got[:rows].astype(F32) + far.astype(F32)


def reduce_dp(pack, size):
    place = lax.axis_index("dp")
    bits = []
    bit = 1
    while bit < size:
        bits.append(bit)
        bit *= 2
    for bit in bits:
        half = pack.shape[0] // 2
        mine = (place // bit) % 2
        send = lax.dynamic_slice_in_dim(pack, (1 - mine) * half, half, 0)
        keep = lax.dynamic_slice_in_dim(pack, mine * half, half, 0)
        got = swap(send, "dp", bit, size)
        pack = (keep.astype(F32) + got.astype(F32)).astype(BF)
    for bit in reversed(bits):
        mine = (place // bit) % 2
        got = swap(pack, "dp", bit, size)
        pack = jnp.where(
            mine == 0, jnp.concatenate([pack, got], 0), jnp.concatenate([got, pack], 0)
        )
    return pack


def make_local(dp_size):
    def local(
        tokens,
        out_grad,
        segments,
        neighbours,
        norm_gains,
        norm_biases,
        self_qkv,
        self_out,
        cross_q,
        cross_kv,
        cross_out,
        mlp_in,
        mlp_in_bias,
        mlp_out,
        mlp_out_bias,
    ):
        t = lax.axis_index("tensor")
        rows, width = tokens.shape
        seq_len = 4 * rows
        local_width = self_out.shape[0]
        heads = local_width // HEAD_DIM
        gains = norm_gains.astype(F32)
        biases = norm_biases.astype(F32)
        segment = segments[0]

        def to_absolute(blocks):
            pairs = jnp.where(
                t % 2 == 0,
                jnp.concatenate([jnp.stack(blocks[:2]), jnp.stack(blocks[2:])], 0),
                jnp.concatenate([jnp.stack(blocks[1::-1]), jnp.stack(blocks[3:1:-1])], 0),
            )
            turned = jnp.where(t // 2 == 0, pairs, jnp.concatenate([pairs[2:], pairs[:2]], 0))
            return turned.reshape((-1,) + turned.shape[2:])

        def block_of(whole, j):
            return lax.dynamic_slice_in_dim(whole, (t ^ j) * rows, rows, 0)

        token_blocks = gather_blocks(tokens)
        kv_pack = jnp.concatenate([cross_kv[0].T, cross_kv[1].T], 0)
        kv_full = jnp.stack(gather_blocks(kv_pack)).reshape(4, 2, heads, HEAD_DIM, width)
        rest_pack = jnp.concatenate([self_out, cross_q.T, cross_out], 0)
        rest_full = jnp.stack(gather_blocks(rest_pack)).reshape(4, 3, local_width, width)
        so_full = rest_full[:, 0].reshape(width, width)
        cq_full = rest_full[:, 1].reshape(width, width)
        co_full = rest_full[:, 2].reshape(width, width)
        grads_whole = jnp.concatenate(gather_blocks(out_grad), 0)

        whole_tokens = to_absolute(token_blocks)
        normed_one, _ = norm_rows(whole_tokens.astype(F32))
        input_one = (normed_one * gains[0] + biases[0]).astype(BF)
        projected = jnp.einsum("sd,kde->kse", input_one, self_qkv, preferred_element_type=F32)
        cosine, sine = rope_tables(seq_len)
        shape = (seq_len, heads, HEAD_DIM)
        queries = rotate(projected[0].reshape(shape), cosine, sine).astype(BF)
        keys = rotate(projected[1].reshape(shape), cosine, sine).astype(BF)
        values = projected[2].reshape(shape).astype(BF)
        places = jnp.arange(seq_len)
        allowed = (places[:, None] >= places[None, :]) & (segment[:, None] == segment[None, :])

        def self_scores():
            scores = jnp.einsum("qhe,khe->hqk", queries, keys, preferred_element_type=F32) * 0.125
            return jnp.where(allowed[None], scores, MASKED)

        scores = self_scores()
        row_max = jnp.max(scores, -1, keepdims=True)
        expo = jnp.exp(scores - row_max)
        row_sum = jnp.sum(expo, -1, keepdims=True)
        self_lse = row_max + jnp.log(row_sum)
        attended_heads = jnp.einsum(
            "hqk,khe->qhe", (expo / row_sum).astype(BF), values, preferred_element_type=F32
        ).astype(BF).reshape(seq_len, local_width)
        attended = jnp.concatenate(
            [block_of(attended_heads, 0)]
            + [swap(block_of(attended_heads, j), "tensor", j, 4) for j in (1, 2, 3)],
            1,
        )

        resid_one = tokens.astype(F32) + nn(attended, so_full)
        normed_two, inverse_two = norm_rows(resid_one)
        input_two = (normed_two * gains[1] + biases[1]).astype(BF)
        cross_queries = nt(input_two, cq_full).astype(BF)
        sets = neighbours.shape[0] // 4
        nb_tokens = neighbours.shape[1]
        before = lax.dynamic_slice_in_dim(neighbours, jnp.maximum(sets * t - 1, 0), 1, 0)
        own_sets = jnp.concatenate(
            [before, lax.dynamic_slice_in_dim(neighbours, sets * t, sets, 0)], 0
        )
        groups = sets + 1
        pool = jnp.einsum(
            "pnd,jkhed->kpnjhe", own_sets, kv_full, preferred_element_type=F32
        ).astype(BF).reshape(2, groups, nb_tokens, 4 * heads, HEAD_DIM)
        tail = SPAN * groups - rows - 1
        span_rows = (jnp.arange(groups * SPAN) >= jnp.where(t == 0, SPAN, 1)) & (
            jnp.arange(groups * SPAN) < rows + 1
        )

        def to_spans(array):
            padded = jnp.pad(array, ((1, tail), (0, 0)))
            padded = jnp.where(span_rows[:, None], padded, jnp.zeros((), array.dtype))
            return padded.reshape(groups, SPAN, 4 * heads, HEAD_DIM)

        def from_spans(array):
            flat = array.reshape(groups * SPAN, width)
            return jnp.where(span_rows[:, None], flat, jnp.zeros((), flat.dtype))[1 : rows + 1]

        shifted = to_spans(cross_queries)
        cross_scores = (
            jnp.einsum("cqhe,cnhe->chqn", shifted, pool[0], preferred_element_type=F32) * 0.125
        )
        cross_max = jnp.max(cross_scores, -1, keepdims=True)
        cross_expo = jnp.exp(cross_scores - cross_max)
        cross_probs = cross_expo / jnp.sum(cross_expo, -1, keepdims=True)
        cross_low = cross_probs.astype(BF)
        cross_mixed = jnp.einsum(
            "chqn,cnhe->cqhe", cross_low, pool[1], preferred_element_type=F32
        ).astype(BF)
        cross_mixed = from_spans(cross_mixed)
        resid_two = resid_one + nn(cross_mixed, co_full)
        normed_three, inverse_three = norm_rows(resid_two)
        input_three = (normed_three * gains[2] + biases[2]).astype(BF)

        mlp_rows = jnp.concatenate(gather_blocks(input_three), 0)
        pre_act = nn(mlp_rows, mlp_in) + mlp_in_bias.astype(F32)
        hidden, gelu_pull = jax.vjp(gelu_tanh, pre_act)
        hidden = hidden.astype(BF)
        grad_hidden = nt(grads_whole, mlp_out)
        grad_pre = gelu_pull(grad_hidden)[0].astype(BF)
        part_three = nt(grad_pre, mlp_in).astype(BF).reshape(4, rows, width)
        grad_norm_three = scatter_sum(part_three)
        branch_three = nn(hidden, mlp_out).astype(BF).reshape(4, rows, width)
        branch_three = scatter_sum(branch_three)
        output = (resid_two + branch_three + mlp_out_bias.astype(F32)).astype(BF)
        grad_mlp_out = reduce_dp(tn(hidden, grads_whole).astype(BF), dp_size)
        grad_mlp_in = reduce_dp(tn(mlp_rows, grad_pre).astype(BF), dp_size)
        bias_in_part = jnp.sum(grad_pre, 0, dtype=F32)
        bias_out_part = jnp.sum(out_grad, 0, dtype=F32)

        grads_two = out_grad.astype(F32) + norm_back(
            grad_norm_three, normed_three, inverse_three, gains[2]
        )
        grads_two_low = grads_two.astype(BF)
        co_part = tn(cross_mixed, grads_two_low)
        grad_mixed = to_spans(nt(grads_two_low, co_full).astype(BF))
        grad_probs = jnp.einsum(
            "cqhe,cnhe->chqn", grad_mixed, pool[1], preferred_element_type=F32
        )
        inner = jnp.sum(cross_probs * grad_probs, -1, keepdims=True)
        grad_scores = (cross_probs * (grad_probs - inner)).astype(BF)
        grad_queries = (
            jnp.einsum("chqn,cnhe->cqhe", grad_scores, pool[0], preferred_element_type=F32) * 0.125
        )
        grad_queries = from_spans(grad_queries.astype(BF))
        grad_norm_two = nn(grad_queries, cq_full)
        grads_one = grads_two + norm_back(grad_norm_two, normed_two, inverse_two, gains[1])
        grads_one_low = grads_one.astype(BF)
        grad_attended = nt(grads_one_low, so_full).astype(BF).reshape(rows, 4, local_width)

        upstream = to_absolute(
            [grad_attended[:, 0]]
            + [swap(grad_attended[:, j], "tensor", j, 4) for j in (1, 2, 3)]
        ).reshape(shape)
        probs = jnp.exp(self_scores() - self_lse)
        grad_self_probs = jnp.einsum("qhe,khe->hqk", upstream, values, preferred_element_type=F32)
        self_inner = jnp.sum(probs * grad_self_probs, -1, keepdims=True)
        grad_self_scores = (probs * (grad_self_probs - self_inner)).astype(BF)
        query_grads = (
            jnp.einsum("hqk,khe->qhe", grad_self_scores, keys, preferred_element_type=F32) * 0.125
        )
        key_grads = (
            jnp.einsum("hqk,qhe->khe", grad_self_scores, queries, preferred_element_type=F32)
            * 0.125
        )
        value_grads = jnp.einsum(
            "hqk,qhe->khe", probs.astype(BF), upstream, preferred_element_type=F32
        )
        grad_projected = jnp.stack(
            [
                rotate(query_grads, cosine, -sine).astype(BF),
                rotate(key_grads, cosine, -sine).astype(BF),
                value_grads.astype(BF),
            ]
        ).reshape(3, seq_len, local_width)
        qkv_part = jnp.einsum("sd,kse->ked", input_one, grad_projected, preferred_element_type=F32)
        grad_qkv = reduce_dp(qkv_part.astype(BF).reshape(3 * local_width, width), dp_size)
        grad_self_qkv = grad_qkv.reshape(3, local_width, width).transpose(0, 2, 1).astype(F32)
        part_one = jnp.einsum(
            "kse,kde->sd", grad_projected, self_qkv, preferred_element_type=F32
        ).astype(BF)
        grad_norm_one = scatter_sum([block_of(part_one, j) for j in range(4)])
        own_normed, own_inverse = norm_rows(tokens.astype(F32))
        tokens_grad = (
            grads_one + norm_back(grad_norm_one, own_normed, own_inverse, gains[0])
        ).astype(BF)

        grad_keys = (
            jnp.einsum("chqn,cqhe->cnhe", grad_scores, shifted, preferred_element_type=F32) * 0.125
        )
        grad_values = jnp.einsum(
            "chqn,cqhe->cnhe", cross_low, grad_mixed, preferred_element_type=F32
        )
        grad_pool = (
            jnp.stack([grad_keys, grad_values])
            .astype(BF)
            .reshape(2, groups, nb_tokens, 4, heads, HEAD_DIM)
        )
        kv_part = jnp.einsum(
            "pnd,kpnjhe->jkhed", own_sets, grad_pool, preferred_element_type=F32
        ).reshape(4, 2 * local_width, width)
        nb_part = jnp.einsum("kpnjhe,jkhed->pnd", grad_pool, kv_full, preferred_element_type=F32)
        back = lax.ppermute(nb_part[0].astype(BF), "tensor", [(i + 1, i) for i in range(3)])
        last = nb_part[sets] + back.astype(F32)
        neighbours_grad = jnp.concatenate([nb_part[1:sets], last[None]], 0).astype(BF)
        cq_part = tn(grad_queries, input_two).reshape(4, local_width, width)
        so_part = tn(attended, grads_one_low).reshape(4, local_width, width)
        co_part = co_part.reshape(4, local_width, width)
        parts = jnp.concatenate([so_part, co_part, cq_part, kv_part], 1).astype(BF)
        own_part = reduce_dp(scatter_sum(parts).astype(BF), dp_size).astype(F32)
        own_part = own_part.reshape(5, local_width, width)
        grad_self_out = own_part[0]
        grad_cross_out = own_part[1]
        grad_cross_q = own_part[2].T
        grad_cross_kv = own_part[3:].transpose(0, 2, 1)

        small = jnp.stack(
            [
                jnp.sum(grad_norm_one * own_normed, 0),
                jnp.sum(grad_norm_two * normed_two, 0),
                jnp.sum(grad_norm_three * normed_three, 0),
                jnp.sum(grad_norm_one, 0),
                jnp.sum(grad_norm_two, 0),
                jnp.sum(grad_norm_three, 0),
                bias_out_part,
            ]
        )
        small = small + core_swap(small)
        small = small + x_swap(small)
        small = jnp.concatenate([small, bias_in_part[None]], 0)
        bit = 1
        while bit < dp_size:
            small = small + swap(small, "dp", bit, dp_size)
            bit *= 2
        return (
            output,
            tokens_grad,
            neighbours_grad,
            small[:3],
            small[3:6],
            grad_self_qkv,
            grad_self_out,
            grad_cross_q,
            grad_cross_kv,
            grad_cross_out,
            grad_mlp_in.astype(F32),
            small[7],
            grad_mlp_out.astype(F32),
            small[6],
        )

    return local


def solution(mesh):
    rows = P(("dp", "tensor"), None)
    in_specs = (
        rows,
        rows,
        P("dp", None),
        P("dp", None, None),
        P(),
        P(),
        P(None, None, "tensor"),
        P("tensor", None),
        P(None, "tensor"),
        P(None, None, "tensor"),
        P("tensor", None),
        P(None, "tensor"),
        P("tensor"),
        P("tensor", None),
        P(),
    )
    out_specs = (
        rows,
        rows,
        P(("dp", "tensor"), None, None),
        P(),
        P(),
        P(None, None, "tensor"),
        P("tensor", None),
        P(None, "tensor"),
        P(None, None, "tensor"),
        P("tensor", None),
        P(None, "tensor"),
        P("tensor"),
        P("tensor", None),
        P(),
    )
    return jax.shard_map(
        make_local(mesh.shape["dp"]),
        mesh=mesh,
        in_specs=in_specs,
        out_specs=out_specs,
        check_vma=False,
    )
```

time: 834 us -> 408 us (0.49)
  waiting for transfers between devices: 545 us -> 134 us
  starting transfers between devices: 1.68 us -> 63.6 us
  blocking collectives: 59.9 us -> 0 us
  matrix products: 114 us -> 95 us
  local copies, waits for them, and re-layouts: 40 us -> 53 us
  between operations: 15.4 us -> 3.12 us
  other arithmetic: 43.6 us -> 55.2 us
    psum x1 -> x0, waiting for transfers between devices: 302 us -> none  [local(): lax.psum((grad_self_qkv, grad_self_out, grad_mlp_in, grad_mlp_in_bias, gr...]
    reduce_scatter x7 -> x0, waiting for transfers between devices: 137 us -> none  [the longest x1 29.5 us: local(): lax.psum_scatter(jnp.dot(hidden, mlp_out, preferred_element_type=wide_typ...]
    ppermute x0 -> x59, waiting for transfers between devices: none -> 134 us  [the longest x58 134 us: swap(): return lax.ppermute(value, axis, [(i, i ^ bit) for i in range(size)])]
    all_gather x6 -> x0, waiting for transfers between devices: 104 us -> none  [the longest x1 21.4 us: local(): lax.all_gather(tokens, 'tensor', axis=0, tiled=True)]
    ppermute x0 -> x59, starting transfers between devices: none -> 63.6 us  [the longest x58 62.3 us: swap(): return lax.ppermute(value, axis, [(i, i ^ bit) for i in range(size)])]
    psum x2 -> x0, blocking collectives: 59.9 us -> none  [the longest x1 37.7 us: local(): lax.psum((gain_parts, bias_parts), ('dp', 'tensor'))]
    dot_general x39 -> x31, matrix products: 111 us -> 92.4 us  [the longest x1 11.7 us: local(): jnp.einsum('chqn,cnhe->cqhe', cross_low, pool[1], preferred_element_type=...]
    reduce_sum x10 -> x7, other arithmetic: 14.1 us -> 5.05 us  [the longest x1 1.75 us: local(): row_sum = jnp.sum(expo, -1, keepdims=True)]
  transfers between devices with their start and end apart: 14 -> 59, of which waited for: 12 -> 21; matrix products, arithmetic and copies ran while one was open for 7% -> 43% of each run, Pallas kernels for 0% -> 0%
where the time goes in v1:
time: 408 us; the launch traced here: 404 us
  waiting for transfers between devices  134 us (33%)
  matrix products  95 us (23%)
  starting transfers between devices  63.6 us (16%)
  other arithmetic  55.2 us (14%)
  local copies, waits for them, and re-layouts  53 us (13%)
    ppermute x58, waiting for transfers between devices, swap(): return lax.ppermute(value, axis, [(i, i ^ bit) for i in range(size)])  134 us
    ppermute x58, starting transfers between devices, swap(): return lax.ppermute(value, axis, [(i, i ^ bit) for i in range(size)])  62.3 us
    unnamed x221, local copies, waits for them, and re-layouts  13.3 us
    dot_general x1, matrix products, local(): jnp.einsum('chqn,cnhe->cqhe', cross_low, pool[1], preferred_element_type=...  11.7 us
    dot_general x1, matrix products, local(): jnp.einsum('chqn,cqhe->cnhe', cross_low, grad_mixed, preferred_element_ty...  11.4 us
    dot_general x5, matrix products, nn(): return jnp.dot(left, right, preferred_element_type=F32)  9.46 us
    reshape x4, local copies, waits for them, and re-layouts, to_spans(): return padded.reshape(groups, SPAN, 4 * heads, HEAD_DIM)  8.63 us
    dot_general x5, matrix products, tn(): lax.dot_general(left, right, (((0,), (0,)), ((), ())), preferred_element_...  8.34 us
  transfers between devices with their start and end apart: 59, of which 21 were waited for; matrix products, arithmetic and copies ran while one was open for 43% of the time, Pallas kernels for 0%

profile of v1, /device:TPU:0, one launch (start us, length us, event | category | flops | bytes accessed | tf_op | source)
XLA Modules:
  0.0 404.0 jit_solution(15852601549256118747)
XLA Ops:
  1.2 2.6 collective-permute-start.18
  9.1 2.7 constant_dynamic-slice_fusion.14
  16.3 6.1 %collective-permute-done.1 = bf16[256,768]{1,0:T(8,128)(2,1)S(1)} collective-permute-done((bf16[256,768]{1,0:T(8,128)(2,1)}, bf16[256,768]{1,0:T(8,128)(2,1)S(1)}, u32[]{:S(2)}, u32[]{:S(2)}) %collective-permute-start.1) | collective-permute-done | bytes 393248 | tf_op jit(solution)/shard_map/ppermute | solution.py:62
  24.2 10.7 %collective-permute-done.10 = bf16[384,768]{1,0:T(8,128)(2,1)} collective-permute-done((bf16[384,768]{1,0:T(8,128)(2,1)}, bf16[384,768]{1,0:T(8,128)(2,1)}, u32[]{:S(2)}, u32[]{:S(2)}) %collective-permute-start.10) | collective-permute-done | bytes 589856 | tf_op jit(solution)/shard_map/ppermute | solution.py:62
  43.5 2.6 fusion.144
  47.9 2.8 copy-done.2
  54.0 2.4 collective-permute-done.7
  58.0 4.9 %convert_bitcast_fusion = bf16[2,5,256,4,3,64]{2,5,1,4,0,3:T(8,128)(2,1)S(1)} fusion(bf16[4,256,768]{2,1,0:T(8,128)(2,1)S(1)} %copy-done.22, bf16[1,256,768]{2,1,0:T(8,128)(2,1)S(1)} %copy-done.44, bf16[1,2,3,64,768]{4,3,2,1,0:T(8,128)(2,1)} %bitcast.30, bf16[1,2,3,64,768]{4,3,2,1,0:T(8,128)(2,1)} %bitcast.29, bf16[1,2,3,64,768]{4,3,2,1,0:T(8,128)(2,1)} %bitcast.28, ...), kind=kOutput, calls=%fused_computation.27 | convolution fusion | flops 3035234304 | bytes 8257536 | tf_op jit(solution)/shard_map/pnd,jkhed->kpnjhe/dot_general | solution.py:200
  73.9 2.5 copy.85
  76.4 2.6 fusion.48
  79.0 3.0 fusion.146
  82.1 11.7 %fusion.62 = bf16[5,64,12,64]{1,3,2,0:T(8,128)(2,1)} fusion(bf16[5,256,12,64]{1,3,0,2:T(8,128)(2,1)} %bitcast.226, f32[5,12,64]{2,1,0:T(8,128)S(1)} %get-tuple-element.97, f32[5,12,64,256]{3,2,1,0:T(8,128)} %copy-done.5), kind=kOutput, calls=%fused_computation.97 | convolution fusion | flops 130994176 | bytes 6405120 | tf_op jit(solution)/shard_map/chqn,cnhe->cqhe/dot_general | solution.py:225
  93.7 2.7 copy.75
  96.4 2.9 reshape.430
  105.3 7.4 %collective-permute-done.13 = bf16[256,768]{1,0:T(8,128)(2,1)} collective-permute-done((bf16[256,768]{1,0:T(8,128)(2,1)S(1)}, bf16[256,768]{1,0:T(8,128)(2,1)}, u32[]{:S(2)}, u32[]{:S(2)}) %collective-permute-start.13) | collective-permute-done | bytes 393248 | tf_op jit(solution)/shard_map/ppermute | solution.py:62
  114.8 2.4 fusion.94
  119.2 3.7 convert_reduce_fusion
  126.4 2.5 convolution_convert_fusion.4
  132.5 12.7 %collective-permute-done.53 = bf16[384,768]{1,0:T(8,128)(2,1)S(1)} collective-permute-done((bf16[384,768]{1,0:T(8,128)(2,1)S(1)}, bf16[384,768]{1,0:T(8,128)(2,1)S(1)}, u32[]{:S(2)}, u32[]{:S(2)}) %collective-permute-start.53) | collective-permute-done | bytes 589856 | tf_op jit(solution)/shard_map/ppermute | solution.py:62
  147.1 10.4 %collective-permute-done.47 = bf16[384,768]{1,0:T(8,128)(2,1)S(1)} collective-permute-done((bf16[384,768]{1,0:T(8,128)(2,1)S(1)}, bf16[384,768]{1,0:T(8,128)(2,1)S(1)}, u32[]{:S(2)}, u32[]{:S(2)}) %collective-permute-start.47) | collective-permute-done | bytes 589856 | tf_op jit(solution)/shard_map/ppermute | solution.py:62
  160.5 2.7 collective-permute-start.55
  163.2 6.4 %collective-permute-done.48 = bf16[192,768]{1,0:T(8,128)(2,1)S(1)} collective-permute-done((bf16[192,768]{1,0:T(8,128)(2,1)S(1)}, bf16[192,768]{1,0:T(8,128)(2,1)S(1)}, u32[]{:S(2)}, u32[]{:S(2)}) %collective-permute-start.48) | collective-permute-done | bytes 294944 | tf_op jit(solution)/shard_map/ppermute | solution.py:62
  172.8 9.9 %collective-permute-done.49 = bf16[96,768]{1,0:T(8,128)(2,1)S(1)} collective-permute-done((bf16[96,768]{1,0:T(8,128)(2,1)S(1)}, bf16[96,768]{1,0:T(8,128)(2,1)S(1)}, u32[]{:S(2)}, u32[]{:S(2)}) %collective-permute-start.49) | collective-permute-done | bytes 147488 | tf_op jit(solution)/shard_map/ppermute | solution.py:62
  186.0 2.5 collective-permute-start.57
  188.5 2.7 collective-permute-done.50
  199.6 2.5 copy.86
  202.1 11.4 %convolution_convert_fusion = bf16[5,12,64,256]{3,2,1,0:T(8,128)(2,1)} fusion(bf16[5,64,12,64]{1,3,2,0:T(8,128)(2,1)S(1)} %copy.86, f32[5,12,64]{2,1,0:T(8,128)S(1)} %copy-done.47, f32[5,12,64,256]{3,2,1,0:T(8,128)} %copy-done.5), kind=kOutput, calls=%fused_computation.64 | convolution fusion | flops 131731456 | bytes 6405120 | tf_op jit(solution)/shard_map/chqn,cqhe->cnhe/dot_general | solution.py:309
  213.6 4.4 %multiply_reduce_fusion.1 = (f32[5,12,64]{2,1,0:T(8,128)S(1)}, f32[5,12,64,256]{3,2,1,0:T(8,128)S(1)}) fusion(f32[5,12,64,256]{3,2,1,0:T(8,128)} %get-tuple-element.98, f32[5,12,64]{2,1,0:T(8,128)S(1)} %copy-done.47, bf16[5,64,12,64]{1,3,2,0:T(8,128)(2,1)S(1)} %copy.86, bf16[5,256,12,64]{1,3,0,2:T(8,128)(2,1)} %bitcast.227), kind=kOutput, calls=%fused_computation.25 | convolution fusion | flops 128774400 | bytes 10352640 | tf_op jit(solution)/shard_map/cqhe,cnhe->chqn/dot_general | solution.py:255
  223.2 2.7 copy.79
  225.9 2.7 reshape.432
  228.7 2.5 multiply_reduce_fusion.5
  233.0 4.6 %fusion.29 = bf16[4,2,3,64,768]{4,3,1,2,0:T(8,128)(2,1)} fusion(bf16[4,256,768]{2,1,0:T(8,128)(2,1)S(1)} %copy-done.23, bf16[1,256,768]{2,1,0:T(8,128)(2,1)S(1)} %copy-done.45, bf16[1,5,256,4,3,64]{2,5,4,3,1,0:T(8,128)(2,1)S(1)} %bitcast.261, bf16[1,5,256,4,3,64]{2,5,4,3,1,0:T(8,128)(2,1)S(1)} %bitcast.224), kind=kOutput, calls=%fused_computation.53 | convolution fusion | flops 3024027648 | bytes 8257536 | tf_op jit(solution)/shard_map/pnd,kpnjhe->jkhed/dot_general | solution.py:317
  237.7 7.5 %fusion.148 = (bf16[5,256,768]{2,1,0:T(8,128)(2,1)}, f32[5,256,768]{2,1,0:T(8,128)}) fusion(bf16[1,2,3,64,768]{4,3,2,1,0:T(8,128)(2,1)} %bitcast.30, bf16[1,2,3,64,768]{4,3,2,1,0:T(8,128)(2,1)} %bitcast.29, bf16[1,2,3,64,768]{4,3,2,1,0:T(8,128)(2,1)} %bitcast.28, bf16[1,2,3,64,768]{4,3,2,1,0:T(8,128)(2,1)} %bitcast.27, ...), kind=kOutput, calls=%fused_computation.309 | convolution fusion | flops 3026386944 | bytes 12189696 | tf_op jit(solution)/shard_map/kpnjhe,jkhed->pnd/dot_general | solution.py:320
  263.6 5.9 %multiply_reduce_fusion = (f32[3,1024]{1,0:T(4,128)S(1)}, f32[3,1024,1024]{1,2,0:T(8,128)S(1)}) fusion(f32[3,1024,1024]{1,2,0:T(8,128)} %copy-done.2, f32[3,1024]{1,0:T(4,128)S(1)} %log_add_fusion, bf16[1024,3,64]{0,2,1:T(8,128)(2,1)S(1)} %select_n.347, bf16[1024,3,64]{0,2,1:T(8,128)(2,1)S(1)} %bitcast.223), kind=kOutput, calls=%fused_computation.2 | convolution fusion | flops 412087296 | bytes 25976832 | tf_op jit(solution)/shard_map/qhe,khe->hqk/dot_general | solution.py:274
  269.6 7.9 %multiply_convert_fusion = bf16[3,1024,1024]{1,2,0:T(8,128)(2,1)S(1)} fusion(f32[3,1024,1024]{1,2,0:T(8,128)S(1)} %get-tuple-element.105, f32[3,1024,1024]{1,2,0:T(8,128)} %copy-done.2, f32[3,1024]{1,0:T(4,128)S(1)} %get-tuple-element.104, f32[3,1024]{1,0:T(4,128)S(1)} %log_add_fusion), kind=kLoop, calls=%fused_computation.1 | loop fusion | flops 12582912 | bytes 31481856 | tf_op jit(solution)/shard_map/convert_element_type | solution.py:276
  294.6 2.8 collective-permute-done.33
  299.2 2.8 collective-permute-start.34
  306.0 2.4 collective-permute-start.35
  308.4 15.0 %collective-permute-done.40 = bf16[960,768]{1,0:T(8,128)(2,1)S(1)} collective-permute-done((bf16[960,768]{1,0:T(8,128)(2,1)S(1)}, bf16[960,768]{1,0:T(8,128)(2,1)S(1)}, u32[]{:S(2)}, u32[]{:S(2)}) %collective-permute-start.40) | collective-permute-done | bytes 1474592 | tf_op jit(solution)/shard_map/ppermute | solution.py:62
  326.3 3.1 collective-permute-start.36
  334.9 7.9 %collective-permute-done.41 = bf16[480,768]{1,0:T(8,128)(2,1)S(1)} collective-permute-done((bf16[480,768]{1,0:T(8,128)(2,1)S(1)}, bf16[480,768]{1,0:T(8,128)(2,1)S(1)}, u32[]{:S(2)}, u32[]{:S(2)}) %collective-permute-start.41) | collective-permute-done | bytes 737312 | tf_op jit(solution)/shard_map/ppermute | solution.py:62
  343.0 2.8 collective-permute-start.42
  357.0 6.0 %collective-permute-done.43 = bf16[120,768]{1,0:T(8,128)(2,1)S(1)} collective-permute-done((bf16[120,768]{1,0:T(8,128)(2,1)S(1)}, bf16[120,768]{1,0:T(8,128)(2,1)S(1)}, u32[]{:S(2)}, u32[]{:S(2)}) %collective-permute-start.43) | collective-permute-done | bytes 184352 | tf_op jit(solution)/shard_map/ppermute | solution.py:62
  363.2 2.3 collective-permute-start.31
  365.5 6.8 %collective-permute-done.44 = bf16[120,768]{1,0:T(8,128)(2,1)S(1)} collective-permute-done((bf16[120,768]{1,0:T(8,128)(2,1)S(1)}, bf16[120,768]{1,0:T(8,128)(2,1)S(1)}, u32[]{:S(2)}, u32[]{:S(2)}) %collective-permute-start.44) | collective-permute-done | bytes 184352 | tf_op jit(solution)/shard_map/ppermute | solution.py:62
  372.5 2.8 collective-permute-start.32
  376.4 4.8 %collective-permute-done.32 = f32[8,768]{1,0:T(8,128)S(1)} collective-permute-done((f32[8,768]{1,0:T(8,128)S(1)}, f32[8,768]{1,0:T(8,128)S(1)}, u32[]{:S(2)}, u32[]{:S(2)}) %collective-permute-start.32) | collective-permute-done | bytes 24608 | tf_op jit(solution)/shard_map/ppermute | solution.py:62
  387.8 13.3 %collective-permute-done.46 = bf16[480,768]{1,0:T(8,128)(2,1)S(1)} collective-permute-done((bf16[480,768]{1,0:T(8,128)(2,1)S(1)}, bf16[480,768]{1,0:T(8,128)(2,1)S(1)}, u32[]{:S(2)}, u32[]{:S(2)}) %collective-permute-start.46) | collective-permute-done | bytes 737312 | tf_op jit(solution)/shard_map/ppermute | solution.py:62
  (479 shorter events, 152.7 us)
Async XLA Ops:
  0.7 103.4 %collective-permute-start.17 = (bf16[256,768]{1,0:T(8,128)(2,1)}, bf16[256,768]{1,0:T(8,128)(2,1)}, u32[]{:S(2)}, u32[]{:S(2)}) collective-permute-start(bf16[256,768]{1,0:T(8,128)(2,1)} %param.16), channel_id=1, source_target_pairs={{0,1},{1,0},{2,3},{3,2},{4,5},{5,4},{6,7},{7,6},{8,9},{9,8},{10,11... | collective-permute-start | bytes 1179656 | tf_op jit(solution)/shard_map/ppermute | solution.py:62
  1.2 52.1 %collective-permute-start.18 = (bf16[256,768]{1,0:T(8,128)(2,1)}, bf16[256,768]{1,0:T(8,128)(2,1)}, u32[]{:S(2)}, u32[]{:S(2)}) collective-permute-start(bf16[256,768]{1,0:T(8,128)(2,1)} %param.16), channel_id=1, source_target_pairs={{0,2},{1,3},{2,0},{3,1},{4,6},{5,7},{6,4},{7,5},{8,10},{9,11},{10,... | collective-permute-start | bytes 1179656 | tf_op jit(solution)/shard_map/ppermute | solution.py:62
  3.8 18.6 %collective-permute-start.1 = (bf16[256,768]{1,0:T(8,128)(2,1)}, bf16[256,768]{1,0:T(8,128)(2,1)S(1)}, u32[]{:S(2)}, u32[]{:S(2)}) collective-permute-start(bf16[256,768]{1,0:T(8,128)(2,1)} %param.15), channel_id=1, source_target_pairs={{0,2},{1,3},{2,0},{3,1},{4,6},{5,7},{6,4},{7,5},{8,10},{9,11},{10,... | collective-permute-start | bytes 1179656 | tf_op jit(solution)/shard_map/ppermute | solution.py:62
  3.9 19.8 %collective-permute-start = (bf16[256,768]{1,0:T(8,128)(2,1)}, bf16[256,768]{1,0:T(8,128)(2,1)S(1)}, u32[]{:S(2)}, u32[]{:S(2)}) collective-permute-start(bf16[256,768]{1,0:T(8,128)(2,1)} %param.15), channel_id=1, source_target_pairs={{0,1},{1,0},{2,3},{3,2},{4,5},{5,4},{6,7},{7,6},{8,9},{9,8},{10,11... | collective-permute-start | bytes 1179656 | tf_op jit(solution)/shard_map/ppermute | solution.py:62
  5.9 29.0 %collective-permute-start.10 = (bf16[384,768]{1,0:T(8,128)(2,1)}, bf16[384,768]{1,0:T(8,128)(2,1)}, u32[]{:S(2)}, u32[]{:S(2)}) collective-permute-start(bf16[384,768]{1,0:T(8,128)(2,1)} %pad_maximum_fusion.15), channel_id=1, source_target_pairs={{0,2},{1,3},{2,0},{3,1},{4,6},{5,7},{6,4},{7,5},{8,10},{9,11},{10,... | collective-permute-start | bytes 1769480 | tf_op jit(solution)/shard_map/ppermute | solution.py:62
  22.4 14.2 %collective-permute-start.2 = (bf16[256,768]{1,0:T(8,128)(2,1)S(1)}, bf16[256,768]{1,0:T(8,128)(2,1)}, u32[]{:S(2)}, u32[]{:S(2)}) collective-permute-start(bf16[256,768]{1,0:T(8,128)(2,1)S(1)} %collective-permute-done.1), channel_id=1, source_target_pairs={{0,1},{1,0},{2,3},{3,2},{4,5},{5,4},{6,7},{7,6},{8,9},{9,8},{10,11... | collective-permute-start | bytes 1179656 | tf_op jit(solution)/shard_map/ppermute | solution.py:62
  23.6 30.2 %collective-permute-start.9 = (bf16[384,768]{1,0:T(8,128)(2,1)}, bf16[384,768]{1,0:T(8,128)(2,1)}, u32[]{:S(2)}, u32[]{:S(2)}) collective-permute-start(bf16[384,768]{1,0:T(8,128)(2,1)} %pad_maximum_fusion.15), channel_id=1, source_target_pairs={{0,1},{1,0},{2,3},{3,2},{4,5},{5,4},{6,7},{7,6},{8,9},{9,8},{10,11... | collective-permute-start | bytes 1769480 | tf_op jit(solution)/shard_map/ppermute | solution.py:62
  34.8 21.5 %collective-permute-start.7 = (bf16[576,768]{1,0:T(8,128)(2,1)S(1)}, bf16[576,768]{1,0:T(8,128)(2,1)}, u32[]{:S(2)}, u32[]{:S(2)}) collective-permute-start(bf16[576,768]{1,0:T(8,128)(2,1)S(1)} %pad_maximum_fusion.11), channel_id=1, source_target_pairs={{0,2},{1,3},{2,0},{3,1},{4,6},{5,7},{6,4},{7,5},{8,10},{9,11},{10,... | collective-permute-start | bytes 2654216 | tf_op jit(solution)/shard_map/ppermute | solution.py:62
  36.6 19.8 %collective-permute-start.11 = (bf16[384,768]{1,0:T(8,128)(2,1)}, bf16[384,768]{1,0:T(8,128)(2,1)}, u32[]{:S(2)}, u32[]{:S(2)}) collective-permute-start(bf16[384,768]{1,0:T(8,128)(2,1)} %collective-permute-done.10), channel_id=1, source_target_pairs={{0,1},{1,0},{2,3},{3,2},{4,5},{5,4},{6,7},{7,6},{8,9},{9,8},{10,11... | collective-permute-start | bytes 1769480 | tf_op jit(solution)/shard_map/ppermute | solution.py:62
  53.3 11.8 %collective-permute-start.6 = (bf16[576,768]{1,0:T(8,128)(2,1)S(1)}, bf16[576,768]{1,0:T(8,128)(2,1)S(1)}, u32[]{:S(2)}, u32[]{:S(2)}) collective-permute-start(bf16[576,768]{1,0:T(8,128)(2,1)S(1)} %pad_maximum_fusion.11), channel_id=1, source_target_pairs={{0,1},{1,0},{2,3},{3,2},{4,5},{5,4},{6,7},{7,6},{8,9},{9,8},{10,11... | collective-permute-start | bytes 2654216 | tf_op jit(solution)/shard_map/ppermute | solution.py:62
  53.9 59.8 %collective-permute-start.19 = (bf16[256,768]{1,0:T(8,128)(2,1)}, bf16[256,768]{1,0:T(8,128)(2,1)}, u32[]{:S(2)}, u32[]{:S(2)}) collective-permute-start(bf16[256,768]{1,0:T(8,128)(2,1)} %collective-permute-done.18), channel_id=1, source_target_pairs={{0,1},{1,0},{2,3},{3,2},{4,5},{5,4},{6,7},{7,6},{8,9},{9,8},{10,11... | collective-permute-start | bytes 1179656 | tf_op jit(solution)/shard_map/ppermute | solution.py:62
  56.4 11.4 %collective-permute-start.5 = (bf16[256,192]{0,1:T(8,128)(2,1)S(1)}, bf16[256,192]{0,1:T(8,128)(2,1)S(1)}, u32[]{:S(2)}, u32[]{:S(2)}) collective-permute-start(bf16[256,192]{0,1:T(8,128)(2,1)S(1)} %get-tuple-element.79), channel_id=1, source_target_pairs={{0,3},{1,2},{2,1},{3,0},{4,7},{5,6},{6,5},{7,4},{8,11},{9,10},{10,... | collective-permute-start | bytes 294920 | tf_op jit(solution)/shard_map/ppermute | solution.py:62
  102.3 10.4 %collective-permute-start.13 = (bf16[256,768]{1,0:T(8,128)(2,1)S(1)}, bf16[256,768]{1,0:T(8,128)(2,1)}, u32[]{:S(2)}, u32[]{:S(2)}) collective-permute-start(bf16[256,768]{1,0:T(8,128)(2,1)S(1)} %add_convert_fusion.8), channel_id=1, source_target_pairs={{0,2},{1,3},{2,0},{3,1},{4,6},{5,7},{6,4},{7,5},{8,10},{9,11},{10,... | collective-permute-start | bytes 1179656 | tf_op jit(solution)/shard_map/ppermute | solution.py:62
  105.2 9.6 %collective-permute-start.12 = (bf16[256,768]{1,0:T(8,128)(2,1)S(1)}, bf16[256,768]{1,0:T(8,128)(2,1)S(1)}, u32[]{:S(2)}, u32[]{:S(2)}) collective-permute-start(bf16[256,768]{1,0:T(8,128)(2,1)S(1)} %add_convert_fusion.8), channel_id=1, source_target_pairs={{0,1},{1,0},{2,3},{3,2},{4,5},{5,4},{6,7},{7,6},{8,9},{9,8},{10,11... | collective-permute-start | bytes 1179656 | tf_op jit(solution)/shard_map/ppermute | solution.py:62
  129.0 16.2 %collective-permute-start.53 = (bf16[384,768]{1,0:T(8,128)(2,1)S(1)}, bf16[384,768]{1,0:T(8,128)(2,1)S(1)}, u32[]{:S(2)}, u32[]{:S(2)}) collective-permute-start(bf16[384,768]{1,0:T(8,128)(2,1)S(1)} %constant_dynamic-slice_fusion.2), channel_id=1, source_target_pairs={{0,4},{4,0},{8,12},{12,8},{16,20},{20,16},{24,28},{28,24},{1,5},{5... | collective-permute-start | bytes 1769480 | tf_op jit(solution)/shard_map/ppermute | solution.py:62
  130.6 26.8 %collective-permute-start.47 = (bf16[384,768]{1,0:T(8,128)(2,1)S(1)}, bf16[384,768]{1,0:T(8,128)(2,1)S(1)}, u32[]{:S(2)}, u32[]{:S(2)}) collective-permute-start(bf16[384,768]{1,0:T(8,128)(2,1)S(1)} %constant_dynamic-slice_fusion.5), channel_id=1, source_target_pairs={{0,4},{4,0},{8,12},{12,8},{16,20},{20,16},{24,28},{28,24},{1,5},{5... | collective-permute-start | bytes 1769480 | tf_op jit(solution)/shard_map/ppermute | solution.py:62
  131.3 28.0 %collective-permute-start.20 = (bf16[512,768]{1,0:T(8,128)(2,1)S(1)}, bf16[512,768]{1,0:T(8,128)(2,1)S(1)}, u32[]{:S(2)}, u32[]{:S(2)}) collective-permute-start(bf16[512,768]{1,0:T(8,128)(2,1)S(1)} %pad_maximum_fusion.13), channel_id=1, source_target_pairs={{0,1},{1,0},{2,3},{3,2},{4,5},{5,4},{6,7},{7,6},{8,9},{9,8},{10,11... | collective-permute-start | bytes 2359304 | tf_op jit(solution)/shard_map/ppermute | solution.py:62
  132.0 50.8 %collective-permute-start.15 = (bf16[512,768]{1,0:T(8,128)(2,1)S(1)}, bf16[512,768]{1,0:T(8,128)(2,1)S(1)}, u32[]{:S(2)}, u32[]{:S(2)}) collective-permute-start(bf16[512,768]{1,0:T(8,128)(2,1)S(1)} %pad_maximum_fusion.12), channel_id=1, source_target_pairs={{0,1},{1,0},{2,3},{3,2},{4,5},{5,4},{6,7},{7,6},{8,9},{9,8},{10,11... | collective-permute-start | bytes 2359304 | tf_op jit(solution)/shard_map/ppermute | solution.py:62
  145.4 15.0 %collective-permute-start.54 = (bf16[192,768]{1,0:T(8,128)(2,1)S(1)}, bf16[192,768]{1,0:T(8,128)(2,1)S(1)}, u32[]{:S(2)}, u32[]{:S(2)}) collective-permute-start(bf16[192,768]{1,0:T(8,128)(2,1)S(1)} %constant_dynamic-slice_fusion.1), channel_id=1, source_target_pairs={{0,8},{4,12},{8,0},{12,4},{16,24},{20,28},{24,16},{28,20},{1,9},{5... | collective-permute-start | bytes 884744 | tf_op jit(solution)/shard_map/ppermute | solution.py:62
  157.7 11.9 %collective-permute-start.48 = (bf16[192,768]{1,0:T(8,128)(2,1)S(1)}, bf16[192,768]{1,0:T(8,128)(2,1)S(1)}, u32[]{:S(2)}, u32[]{:S(2)}) collective-permute-start(bf16[192,768]{1,0:T(8,128)(2,1)S(1)} %constant_dynamic-slice_fusion.4), channel_id=1, source_target_pairs={{0,8},{4,12},{8,0},{12,4},{16,24},{20,28},{24,16},{28,20},{1,9},{5... | collective-permute-start | bytes 884744 | tf_op jit(solution)/shard_map/ppermute | solution.py:62
  159.4 32.5 %collective-permute-start.21 = (bf16[256,768]{1,0:T(8,128)(2,1)S(1)}, bf16[256,768]{1,0:T(8,128)(2,1)S(1)}, u32[]{:S(2)}, u32[]{:S(2)}) collective-permute-start(bf16[256,768]{1,0:T(8,128)(2,1)S(1)} %add_convert_fusion.5), channel_id=1, source_target_pairs={{0,2},{1,3},{2,0},{3,1},{4,6},{5,7},{6,4},{7,5},{8,10},{9,11},{10,... | collective-permute-start | bytes 1179656 | tf_op jit(solution)/shard_map/ppermute | solution.py:62
  160.5 10.9 %collective-permute-start.55 = (bf16[96,768]{1,0:T(8,128)(2,1)S(1)}, bf16[96,768]{1,0:T(8,128)(2,1)S(1)}, u32[]{:S(2)}, u32[]{:S(2)}) collective-permute-start(bf16[96,768]{1,0:T(8,128)(2,1)S(1)} %constant_dynamic-slice_fusion), channel_id=1, source_target_pairs={{0,16},{4,20},{8,24},{12,28},{16,0},{20,4},{24,8},{28,12},{1,17},{... | collective-permute-start | bytes 442376 | tf_op jit(solution)/shard_map/ppermute | solution.py:62
  169.7 13.0 %collective-permute-start.49 = (bf16[96,768]{1,0:T(8,128)(2,1)S(1)}, bf16[96,768]{1,0:T(8,128)(2,1)S(1)}, u32[]{:S(2)}, u32[]{:S(2)}) collective-permute-start(bf16[96,768]{1,0:T(8,128)(2,1)S(1)} %constant_dynamic-slice_fusion.3), channel_id=1, source_target_pairs={{0,16},{4,20},{8,24},{12,28},{16,0},{20,4},{24,8},{28,12},{1,17},{... | collective-permute-start | bytes 442376 | tf_op jit(solution)/shard_map/ppermute | solution.py:62
  171.5 13.8 %collective-permute-start.56 = (bf16[96,768]{1,0:T(8,128)(2,1)S(1)}, bf16[96,768]{1,0:T(8,128)(2,1)S(1)}, u32[]{:S(2)}, u32[]{:S(2)}) collective-permute-start(bf16[96,768]{1,0:T(8,128)(2,1)S(1)} %add_convert_fusion.19), channel_id=1, source_target_pairs={{0,16},{4,20},{8,24},{12,28},{16,0},{20,4},{24,8},{28,12},{1,17},{... | collective-permute-start | bytes 442376 | tf_op jit(solution)/shard_map/ppermute | solution.py:62
  183.0 10.0 %collective-permute-start.16 = (bf16[256,768]{1,0:T(8,128)(2,1)S(1)}, bf16[256,768]{1,0:T(8,128)(2,1)S(1)}, u32[]{:S(2)}, u32[]{:S(2)}) collective-permute-start(bf16[256,768]{1,0:T(8,128)(2,1)S(1)} %add_convert_fusion.7), channel_id=1, source_target_pairs={{0,2},{1,3},{2,0},{3,1},{4,6},{5,7},{6,4},{7,5},{8,10},{9,11},{10,... | collective-permute-start | bytes 1179656 | tf_op jit(solution)/shard_map/ppermute | solution.py:62
  186.0 105.1 %collective-permute-start.57 = (bf16[192,768]{1,0:T(8,128)(2,1)}, bf16[192,768]{1,0:T(8,128)(2,1)}, u32[]{:S(2)}, u32[]{:S(2)}) collective-permute-start(bf16[192,768]{1,0:T(8,128)(2,1)} %maximum_select_fusion.14), channel_id=1, source_target_pairs={{0,8},{4,12},{8,0},{12,4},{16,24},{20,28},{24,16},{28,20},{1,9},{5... | collective-permute-start | bytes 884744 | tf_op jit(solution)/shard_map/ppermute | solution.py:62
  191.9 100.7 %collective-permute-start.51 = (bf16[192,768]{1,0:T(8,128)(2,1)}, bf16[192,768]{1,0:T(8,128)(2,1)}, u32[]{:S(2)}, u32[]{:S(2)}) collective-permute-start(bf16[192,768]{1,0:T(8,128)(2,1)} %maximum_select_fusion.13), channel_id=1, source_target_pairs={{0,8},{4,12},{8,0},{12,4},{16,24},{20,28},{24,16},{28,20},{1,9},{5... | collective-permute-start | bytes 884744 | tf_op jit(solution)/shard_map/ppermute | solution.py:62
  247.1 12.8 %collective-permute-start.24 = (bf16[256,192]{0,1:T(8,128)(2,1)S(1)}, bf16[256,192]{0,1:T(8,128)(2,1)S(1)}, u32[]{:S(2)}, u32[]{:S(2)}) collective-permute-start(bf16[256,192]{0,1:T(8,128)(2,1)S(1)} %get-tuple-element.75), channel_id=1, source_target_pairs={{0,3},{1,2},{2,1},{3,0},{4,7},{5,6},{6,5},{7,4},{8,11},{9,10},{10,... | collective-permute-start | bytes 294920 | tf_op jit(solution)/shard_map/ppermute | solution.py:62
  247.2 14.1 %collective-permute-start.23 = (bf16[256,192]{0,1:T(8,128)(2,1)S(1)}, bf16[256,192]{0,1:T(8,128)(2,1)S(1)}, u32[]{:S(2)}, u32[]{:S(2)}) collective-permute-start(bf16[256,192]{0,1:T(8,128)(2,1)S(1)} %get-tuple-element.76), channel_id=1, source_target_pairs={{0,2},{1,3},{2,0},{3,1},{4,6},{5,7},{6,4},{7,5},{8,10},{9,11},{10,... | collective-permute-start | bytes 294920 | tf_op jit(solution)/shard_map/ppermute | solution.py:62
  248.3 14.2 %collective-permute-start.22 = (bf16[256,192]{0,1:T(8,128)(2,1)S(1)}, bf16[256,192]{0,1:T(8,128)(2,1)S(1)}, u32[]{:S(2)}, u32[]{:S(2)}) collective-permute-start(bf16[256,192]{0,1:T(8,128)(2,1)S(1)} %get-tuple-element.77), channel_id=1, source_target_pairs={{0,1},{1,0},{2,3},{3,2},{4,5},{5,4},{6,7},{7,6},{8,9},{9,8},{10,11... | collective-permute-start | bytes 294920 | tf_op jit(solution)/shard_map/ppermute | solution.py:62
  260.0 39.2 %collective-permute-start.27 = (bf16[256,768]{1,0:T(8,128)(2,1)}, bf16[256,768]{1,0:T(8,128)(2,1)}, u32[]{:S(2)}, u32[]{:S(2)}) collective-permute-start(bf16[256,768]{1,0:T(8,128)(2,1)} %slice_bitcast_fusion.6), channel_id=1, source_target_pairs={{1,0},{2,1},{3,2},{5,4},{6,5},{7,6},{9,8},{10,9},{11,10},{13,12},{... | collective-permute-start | bytes 1179656 | tf_op jit(solution)/shard_map/ppermute | solution.py:321
  261.3 26.2 %collective-permute-start.39 = (bf16[1920,768]{1,0:T(8,128)(2,1)}, bf16[1920,768]{1,0:T(8,128)(2,1)}, u32[]{:S(2)}, u32[]{:S(2)}) collective-permute-start(bf16[1920,768]{1,0:T(8,128)(2,1)} %pad_maximum_fusion.3), channel_id=1, source_target_pairs={{0,1},{1,0},{2,3},{3,2},{4,5},{5,4},{6,7},{7,6},{8,9},{9,8},{10,11... | collective-permute-start | bytes 8847368 | tf_op jit(solution)/shard_map/ppermute | solution.py:62
  284.4 12.9 %collective-permute-start.33 = (bf16[288,768]{1,0:T(8,128)(2,1)S(1)}, bf16[288,768]{1,0:T(8,128)(2,1)S(1)}, u32[]{:S(2)}, u32[]{:S(2)}) collective-permute-start(bf16[288,768]{1,0:T(8,128)(2,1)S(1)} %constant_dynamic-slice_fusion.11), channel_id=1, source_target_pairs={{0,4},{4,0},{8,12},{12,8},{16,20},{20,16},{24,28},{28,24},{1,5},{5... | collective-permute-start | bytes 1327112 | tf_op jit(solution)/shard_map/ppermute | solution.py:62
  289.4 34.0 %collective-permute-start.40 = (bf16[960,768]{1,0:T(8,128)(2,1)S(1)}, bf16[960,768]{1,0:T(8,128)(2,1)S(1)}, u32[]{:S(2)}, u32[]{:S(2)}) collective-permute-start(bf16[960,768]{1,0:T(8,128)(2,1)S(1)} %fusion.26), channel_id=1, source_target_pairs={{0,2},{1,3},{2,0},{3,1},{4,6},{5,7},{6,4},{7,5},{8,10},{9,11},{10,... | collective-permute-start | bytes 4423688 | tf_op jit(solution)/shard_map/ppermute | solution.py:62
  291.1 41.4 %collective-permute-start.25 = (bf16[512,768]{1,0:T(8,128)(2,1)S(1)}, bf16[512,768]{1,0:T(8,128)(2,1)S(1)}, u32[]{:S(2)}, u32[]{:S(2)}) collective-permute-start(bf16[512,768]{1,0:T(8,128)(2,1)S(1)} %pad_maximum_fusion.14), channel_id=1, source_target_pairs={{0,1},{1,0},{2,3},{3,2},{4,5},{5,4},{6,7},{7,6},{8,9},{9,8},{10,11... | collective-permute-start | bytes 2359304 | tf_op jit(solution)/shard_map/ppermute | solution.py:62
  292.6 38.3 %collective-permute-start.58 = (bf16[384,768]{1,0:T(8,128)(2,1)S(1)}, bf16[384,768]{1,0:T(8,128)(2,1)S(1)}, u32[]{:S(2)}, u32[]{:S(2)}) collective-permute-start(bf16[384,768]{1,0:T(8,128)(2,1)S(1)} %maximum_select_fusion.8), channel_id=1, source_target_pairs={{0,4},{4,0},{8,12},{12,8},{16,20},{20,16},{24,28},{28,24},{1,5},{5... | collective-permute-start | bytes 1769480 | tf_op jit(solution)/shard_map/ppermute | solution.py:62
  297.4 31.9 %collective-permute-start.52 = (bf16[384,768]{1,0:T(8,128)(2,1)S(1)}, bf16[384,768]{1,0:T(8,128)(2,1)S(1)}, u32[]{:S(2)}, u32[]{:S(2)}) collective-permute-start(bf16[384,768]{1,0:T(8,128)(2,1)S(1)} %maximum_select_fusion.7), channel_id=1, source_target_pairs={{0,4},{4,0},{8,12},{12,8},{16,20},{20,16},{24,28},{28,24},{1,5},{5... | collective-permute-start | bytes 1769480 | tf_op jit(solution)/shard_map/ppermute | solution.py:62
  306.0 20.2 %collective-permute-start.35 = (bf16[72,768]{1,0:T(8,128)(2,1)S(1)}, bf16[72,768]{1,0:T(8,128)(2,1)S(1)}, u32[]{:S(2)}, u32[]{:S(2)}) collective-permute-start(bf16[72,768]{1,0:T(8,128)(2,1)S(1)} %constant_dynamic-slice_fusion.9), channel_id=1, source_target_pairs={{0,16},{4,20},{8,24},{12,28},{16,0},{20,4},{24,8},{28,12},{1,17},{... | collective-permute-start | bytes 331784 | tf_op jit(solution)/shard_map/ppermute | solution.py:62
  325.5 17.3 %collective-permute-start.41 = (bf16[480,768]{1,0:T(8,128)(2,1)S(1)}, bf16[480,768]{1,0:T(8,128)(2,1)S(1)}, u32[]{:S(2)}, u32[]{:S(2)}) collective-permute-start(bf16[480,768]{1,0:T(8,128)(2,1)S(1)} %constant_dynamic-slice_fusion.8), channel_id=1, source_target_pairs={{0,4},{4,0},{8,12},{12,8},{16,20},{20,16},{24,28},{28,24},{1,5},{5... | collective-permute-start | bytes 2211848 | tf_op jit(solution)/shard_map/ppermute | solution.py:62
  332.7 13.1 %collective-permute-start.26 = (bf16[256,768]{1,0:T(8,128)(2,1)S(1)}, bf16[256,768]{1,0:T(8,128)(2,1)S(1)}, u32[]{:S(2)}, u32[]{:S(2)}) collective-permute-start(bf16[256,768]{1,0:T(8,128)(2,1)S(1)} %add_convert_fusion.4), channel_id=1, source_target_pairs={{0,2},{1,3},{2,0},{3,1},{4,6},{5,7},{6,4},{7,5},{8,10},{9,11},{10,... | collective-permute-start | bytes 1179656 | tf_op jit(solution)/shard_map/ppermute | solution.py:62
  334.5 12.0 %collective-permute-start.37 = (bf16[144,768]{1,0:T(8,128)(2,1)S(1)}, bf16[144,768]{1,0:T(8,128)(2,1)}, u32[]{:S(2)}, u32[]{:S(2)}) collective-permute-start(bf16[144,768]{1,0:T(8,128)(2,1)S(1)} %maximum_select_fusion.15), channel_id=1, source_target_pairs={{0,8},{4,12},{8,0},{12,4},{16,24},{20,28},{24,16},{28,20},{1,9},{5... | collective-permute-start | bytes 663560 | tf_op jit(solution)/shard_map/ppermute | solution.py:62
  343.0 9.6 %collective-permute-start.42 = (bf16[240,768]{1,0:T(8,128)(2,1)S(1)}, bf16[240,768]{1,0:T(8,128)(2,1)}, u32[]{:S(2)}, u32[]{:S(2)}) collective-permute-start(bf16[240,768]{1,0:T(8,128)(2,1)S(1)} %constant_dynamic-slice_fusion.7), channel_id=1, source_target_pairs={{0,8},{4,12},{8,0},{12,4},{16,24},{20,28},{24,16},{28,20},{1,9},{5... | collective-permute-start | bytes 1105928 | tf_op jit(solution)/shard_map/ppermute | solution.py:62
  347.7 38.4 %collective-permute-start.38 = (bf16[288,768]{1,0:T(8,128)(2,1)S(1)}, bf16[288,768]{1,0:T(8,128)(2,1)S(1)}, u32[]{:S(2)}, u32[]{:S(2)}) collective-permute-start(bf16[288,768]{1,0:T(8,128)(2,1)S(1)} %maximum_select_fusion.9), channel_id=1, source_target_pairs={{0,4},{4,0},{8,12},{12,8},{16,20},{20,16},{24,28},{28,24},{1,5},{5... | collective-permute-start | bytes 1327112 | tf_op jit(solution)/shard_map/ppermute | solution.py:62
  353.7 9.3 %collective-permute-start.43 = (bf16[120,768]{1,0:T(8,128)(2,1)S(1)}, bf16[120,768]{1,0:T(8,128)(2,1)S(1)}, u32[]{:S(2)}, u32[]{:S(2)}) collective-permute-start(bf16[120,768]{1,0:T(8,128)(2,1)S(1)} %constant_dynamic-slice_fusion.6), channel_id=1, source_target_pairs={{0,16},{4,20},{8,24},{12,28},{16,0},{20,4},{24,8},{28,12},{1,17},{... | collective-permute-start | bytes 552968 | tf_op jit(solution)/shard_map/ppermute | solution.py:62
  363.1 9.3 %collective-permute-start.44 = (bf16[120,768]{1,0:T(8,128)(2,1)S(1)}, bf16[120,768]{1,0:T(8,128)(2,1)S(1)}, u32[]{:S(2)}, u32[]{:S(2)}) collective-permute-start(bf16[120,768]{1,0:T(8,128)(2,1)S(1)} %add_convert_fusion.18), channel_id=1, source_target_pairs={{0,16},{4,20},{8,24},{12,28},{16,0},{20,4},{24,8},{28,12},{1,17},{... | collective-permute-start | bytes 552968 | tf_op jit(solution)/shard_map/ppermute | solution.py:62
  363.2 9.3 %collective-permute-start.31 = (f32[8,768]{1,0:T(8,128)S(1)}, f32[8,768]{1,0:T(8,128)S(1)}, u32[]{:S(2)}, u32[]{:S(2)}) collective-permute-start(f32[8,768]{1,0:T(8,128)S(1)} %fusion.179), channel_id=1, source_target_pairs={{0,8},{4,12},{8,0},{12,4},{16,24},{20,28},{24,16},{28,20},{1,9},{5... | collective-permute-start | bytes 73736 | tf_op jit(solution)/shard_map/ppermute | solution.py:62
  372.4 10.9 %collective-permute-start.45 = (bf16[240,768]{1,0:T(8,128)(2,1)S(1)}, bf16[240,768]{1,0:T(8,128)(2,1)S(1)}, u32[]{:S(2)}, u32[]{:S(2)}) collective-permute-start(bf16[240,768]{1,0:T(8,128)(2,1)S(1)} %maximum_select_fusion.12), channel_id=1, source_target_pairs={{0,8},{4,12},{8,0},{12,4},{16,24},{20,28},{24,16},{28,20},{1,9},{5... | collective-permute-start | bytes 1105928 | tf_op jit(solution)/shard_map/ppermute | solution.py:62
  383.6 17.4 %collective-permute-start.46 = (bf16[480,768]{1,0:T(8,128)(2,1)S(1)}, bf16[480,768]{1,0:T(8,128)(2,1)S(1)}, u32[]{:S(2)}, u32[]{:S(2)}) collective-permute-start(bf16[480,768]{1,0:T(8,128)(2,1)S(1)} %maximum_select_fusion.6), channel_id=1, source_target_pairs={{0,4},{4,0},{8,12},{12,8},{16,20},{20,16},{24,28},{28,24},{1,5},{5... | collective-permute-start | bytes 2211848 | tf_op jit(solution)/shard_map/ppermute | solution.py:62
  (119 other events, 936.2 us)
